TPU v7x, 512 devices: a whole 4x4x16 slice. The times are simulated.
512 devices in a mesh: section: 16 (over x, z_hi), seq: 32 (over z_lo, y, core).
Axes of the slice: x: 4, y: 4, z: 16 (z_hi: 4, z_lo: 4; z = z_hi * 4 + z_lo), core: 2. Of those that a mesh axis runs over, the one named last changes fastest.
Arguments:
- section_states: bfloat16 [16, 2048, 4096], P('section', 'seq'), may hold values from -6 to 6
- dec_states: bfloat16 [16, 512, 4096], P('section', 'seq'), may hold values from -6 to 6
- norm_gain: float32 [16, 4096], P('section'), may hold values from 0.5 to 90
- w_query: bfloat16 [16, 4096, 4096], P('section', None, 'seq'), may hold values from -0.09375 to 0.09375
- w_key: bfloat16 [16, 4096, 4096], P('section', None, 'seq'), may hold values from -0.09375 to 0.09375
- w_value: bfloat16 [16, 4096, 4096], P('section', None, 'seq'), may hold values from -0.09375 to 0.09375
Outputs:
- context: bfloat16 [16, 512, 4096], P('section', 'seq')
All inputs are finite; a program needn't handle non-finite values.
Results may differ from a plain program's by a relative error of at most 0.04.
The roundings to bfloat16 on the way count: a program that leaves them out, or rounds other values in their place, can miss the bound.
Values may be sent and summed in bfloat16 or wider, within the bound.
No kernel may reach another device: no remote copies, remote signals or barrier semaphores. Data moves between devices by JAX's collectives and lax.ppermute only.
A program may use at most 128 MiB of HBM per device.

v0:
```python
import jax
import jax.numpy as jnp
from jax import lax
from jax.sharding import PartitionSpec as P

HD = 256


def broadcast(value, axis, root):
    mine = lax.axis_index(axis) == root
    return lax.psum(jnp.where(mine, value, jnp.zeros_like(value)), axis)


def partner(value, axis, distance):
    mask = 2**distance
    pairs = [(source, source ^ mask) for source in range(lax.axis_size(axis))]
    return lax.ppermute(value, axis, pairs)


def attend(queries, keys_all, values_all, heads_here):
    query_heads = queries.reshape(queries.shape[0], heads_here, HD)
    key_heads = keys_all.reshape(keys_all.shape[0], heads_here, HD)
    value_heads = values_all.reshape(values_all.shape[0], heads_here, HD)
    scores = jnp.einsum(
        "qhd,khd->hqk", query_heads, key_heads, preferred_element_type=jnp.float32
    ) * HD ** (-0.5)
    row_top = jnp.max(scores, axis=-1)
    weights_soft = jnp.exp(scores - row_top[:, :, None]).astype(jnp.bfloat16)
    denom_sum = jnp.sum(weights_soft, axis=-1, dtype=jnp.float32)
    numer_sum = jnp.einsum(
        "hqk,khd->qhd", weights_soft, value_heads, preferred_element_type=jnp.float32
    )
    return (numer_sum, jnp.transpose(row_top), jnp.transpose(denom_sum))


def combine_pair(numer_a, top_a, denom_a, numer_b, top_b, denom_b):
    joint_top = jnp.maximum(top_a, top_b)
    factor_a = jnp.exp(top_a - joint_top)
    factor_b = jnp.exp(top_b - joint_top)
    numer_sum = numer_a * factor_a[..., None] + numer_b * factor_b[..., None]
    denom_sum = denom_a * factor_a + denom_b * factor_b
    return (numer_sum / denom_sum[..., None]).astype(jnp.bfloat16)


def local(section_states, dec_states, norm_gain, w_query, w_key, w_value):
    model_width = dec_states.shape[2]
    dec_count = dec_states.shape[1]
    enc_count = section_states.shape[1]
    seq_count = lax.axis_size("seq")
    seq_index = lax.axis_index("seq")
    half_index = seq_index % 2
    parity_even = half_index == 0
    group_count = seq_count // 2

    def join_halves(mine_part, other_part):
        first_part = jnp.where(parity_even, mine_part, other_part)
        second_part = jnp.where(parity_even, other_part, mine_part)
        return jnp.concatenate([first_part, second_part], axis=1)

    states = dec_states[0].astype(jnp.float32)
    mean_square = jnp.mean(states * states, axis=-1, keepdims=True)
    normed = (states * lax.rsqrt(mean_square + 1e-06) * norm_gain[0]).astype(jnp.bfloat16)
    final_rows = broadcast(section_states, "section", 0)[0]
    mine_cols = (w_query[0], w_key[0], w_value[0])
    other_cols = partner((mine_cols[0], mine_cols[1], mine_cols[2]), "seq", 0)
    query_cols = join_halves(mine_cols[0], other_cols[0])
    key_cols = join_halves(mine_cols[1], other_cols[1])
    value_cols = join_halves(mine_cols[2], other_cols[2])
    group_cols = query_cols.shape[1]
    row_halves = final_rows.reshape(2, enc_count // 2, model_width)
    outgoing_rows = jnp.tile(row_halves, (group_count, 1, 1))[:, None]
    block_rows = lax.all_to_all(outgoing_rows, "seq", split_axis=0, concat_axis=1, tiled=True)
    flat_rows = block_rows.reshape(-1, model_width)
    key_part = jnp.dot(flat_rows, key_cols, preferred_element_type=jnp.float32)
    value_part = jnp.dot(flat_rows, value_cols, preferred_element_type=jnp.float32)
    stacked = jnp.stack([key_part, value_part])
    key_value = stacked.reshape(2, block_rows.shape[1], block_rows.shape[2], group_cols)
    key_value = key_value.astype(jnp.bfloat16).reshape(2, -1, group_cols)
    keys_here = key_value[0]
    values_here = key_value[1]
    heads_here = group_cols // HD
    queries = jnp.dot(
        lax.all_gather(normed, "seq", axis=0, tiled=True),
        query_cols,
        preferred_element_type=jnp.float32,
    ).astype(jnp.bfloat16)
    numer_sum, row_top, denom_sum = attend(queries, keys_here, values_here, heads_here)
    numer_other, top_other, denom_other = partner((numer_sum, row_top, denom_sum), "seq", 0)
    merged = combine_pair(numer_sum, row_top, denom_sum, numer_other, top_other, denom_other)
    merged = merged.reshape(-1, group_cols)
    half_cols = lax.dynamic_slice_in_dim(merged, half_index * (group_cols // 2), group_cols // 2, 1)
    outgoing = half_cols.reshape(seq_count, dec_count, group_cols // 2)
    returned = lax.all_to_all(outgoing, "seq", split_axis=0, concat_axis=2, tiled=True)
    result = returned.reshape(dec_count, model_width)
    return result[None]


def solution(mesh):
    in_specs = (
        P("section", "seq", None),
        P("section", "seq", None),
        P("section", None),
        P("section", None, "seq"),
        P("section", None, "seq"),
        P("section", None, "seq"),
    )
    out_specs = P("section", "seq", None)
    return jax.shard_map(local, mesh=mesh, in_specs=in_specs, out_specs=out_specs, check_vma=False)
```

profile of v0, /device:TPU:1, one launch (start us, length us, event | category | flops | bytes accessed | tf_op | source)
XLA Modules:
  0.0 492.5 jit_solution(638311112740321103)
XLA Ops:
  7.4 0.0 all-reduce.2.cloned.1.call-start
  7.4 1.9 broadcast_select_fusion.6
  9.2 0.0 all-reduce.2.cloned.1.call-update
  9.3 203.7 %all-reduce.2.cloned.1.call-done = bf16[2,32,4096]{2,1,0:T(8,128)(2,1)} async-done(((bf16[2,32,4096]{2,1,0:T(8,128)(2,1)}), bf16[2,32,4096]{2,1,0:T(8,128)(2,1)}) %all-reduce.2.cloned.1.call-update) | async-done | bytes 524304 | tf_op jit(solution)/shard_map/psum | solution.py:11
  212.9 5.3 %tile.10 = bf16[16,2,32,4096]{3,2,1,0:T(8,128)(2,1)} broadcast(bf16[2,32,4096]{2,1,0:T(8,128)(2,1)} %all-reduce.2.cloned.1.call-done), dimensions={1,2,3} | broadcast | bytes 8912896 | tf_op jit(solution)/shard_map/tile | solution.py:71
  218.3 0.0 copy-start.5
  218.3 0.0 copy-start.6
  218.3 0.0 copy-start
  218.3 0.0 copy-start.2
  218.3 0.0 copy-start.1
  218.3 16.7 %all-to-all-start = ((bf16[32,1,32,4096]{3,2,1,0:T(8,128)(2,1)}), bf16[32,1,32,4096]{3,2,1,0:T(8,128)(2,1)}, u32[]{:S(2)}, u32[]{:S(2)}) async-start(bf16[32,1,32,4096]{3,2,1,0:T(8,128)(2,1)} %bitcast.58), calls=%async_computation | async-start | bytes 16777216 | tf_op jit(solution)/shard_map/all_to_all | solution.py:72
  235.0 0.0 all-gather.2.cloned.1.call-start
  235.0 0.0 copy-done.5
  235.1 0.1 fusion.24
  235.2 0.0 copy-done.6
  235.2 0.8 fusion.26
  236.0 0.0 all-gather.2.cloned.1.call-update
  236.0 0.0 copy-done
  236.0 2.3 collective-permute-start.1
  238.3 0.0 copy-done.2
  238.3 2.1 collective-permute-start
  240.4 0.0 copy-done.1
  240.4 2.3 collective-permute-start.2
  242.7 0.0 collective-permute-done.1
  242.7 2.7 broadcast_select_fusion.3
  245.3 0.0 collective-permute-done
  245.3 0.0 collective-permute-done.2
  245.3 3.4 broadcast_select_fusion.1
  248.7 190.9 %all-to-all-done = bf16[32,1,32,4096]{3,2,1,0:T(8,128)(2,1)} async-done(((bf16[32,1,32,4096]{3,2,1,0:T(8,128)(2,1)}), bf16[32,1,32,4096]{3,2,1,0:T(8,128)(2,1)}, u32[]{:S(2)}, u32[]{:S(2)}) %all-to-all-start) | async-done | bytes 8388640 | tf_op jit(solution)/shard_map/all_to_all | solution.py:72
  439.6 0.0 copy-start.4
  439.6 7.1 %fusion.15 = bf16[32,32,256]{2,1,0:T(8,128)(2,1)} fusion(bf16[4096,128]{1,0:T(8,128)(2,1)} %get-tuple-element.11, bf16[4096,128]{1,0:T(8,128)(2,1)} %get-tuple-element.10, bf16[32,1,32,4096]{3,2,1,0:T(8,128)(2,1)} %all-to-all-done), kind=kOutput, calls=%fused_computation.18 | convolution fusion | flops 2151940096 | bytes 11010048 | tf_op jit(solution)/shard_map/dot_general | solution.py:74
  446.8 0.0 copy-done.4
  446.8 0.0 copy-start.3
  446.8 6.6 %fusion.12 = bf16[32,32,256]{2,1,0:T(8,128)(2,1)} fusion(bf16[4096,128]{1,0:T(8,128)(2,1)S(1)} %get-tuple-element.16, bf16[4096,128]{1,0:T(8,128)(2,1)S(1)} %copy-done.4, bf16[32,1,32,4096]{3,2,1,0:T(8,128)(2,1)} %all-to-all-done), kind=kOutput, calls=%fused_computation.17 | convolution fusion | flops 2151940096 | bytes 11010048 | tf_op jit(solution)/shard_map/dot_general | solution.py:75
  453.4 0.0 all-gather.2.cloned.1.call-done
  453.4 0.0 copy-done.3
  453.4 4.7 multiply_reduce_fusion
  458.1 1.6 convolution_bitcast_fusion
  459.8 2.8 collective-permute-start.4
  462.6 0.5 convert_reduce_fusion
  463.1 1.9 collective-permute-start.5
  465.0 2.4 collective-permute-start.3
  467.4 0.0 collective-permute-done.5
  467.4 0.8 collective-permute-done.3
  468.2 0.0 collective-permute-done.4
  468.2 0.1 fusion.29
  468.3 0.1 copy.10
  468.4 16.0 %all_to_all.27 = bf16[32,16,128]{2,1,0:T(8,128)(2,1)S(1)} all-to-all(bf16[32,16,128]{2,1,0:T(8,128)(2,1)S(1)} %bitcast.63), channel_id=1, replica_groups=mesh['section'=16,'seq'=32] {'seq'}, dimensions={0} | all-to-all | bytes 262144 | tf_op jit(solution)/shard_map/all_to_all | solution.py:93
  484.4 0.7 copy_bitcast_fusion
  (2 shorter events, 0.0 us)
Async XLA Ops:
  7.4 205.6 %all-reduce.2.cloned.1.call-start = ((), (), s32[]{:S(2)}) async-start(), calls=%async_computation.2 | async-start | bytes 1048576 | tf_op jit(solution)/shard_map/psum | solution.py:11
  218.3 16.8 %copy-start.5 = (bf16[1,16,4096]{2,1,0:T(8,128)(2,1)S(1)}, bf16[1,16,4096]{2,1,0:T(8,128)(2,1)}, u32[]{:S(2)}) copy-start(bf16[1,16,4096]{2,1,0:T(8,128)(2,1)} %param.7) | copy-start | bytes 393220
  218.3 16.9 %copy-start.6 = (f32[1,4096]{1,0:T(1,128)S(1)}, f32[1,4096]{1,0:T(1,128)}, u32[]{:S(2)}) copy-start(f32[1,4096]{1,0:T(1,128)} %param.8) | copy-start | bytes 49156
  218.3 17.7 %copy-start = (bf16[1,4096,128]{2,1,0:T(8,128)(2,1)S(1)}, bf16[1,4096,128]{2,1,0:T(8,128)(2,1)}, u32[]{:S(2)}) copy-start(bf16[1,4096,128]{2,1,0:T(8,128)(2,1)} %param.9) | copy-start | bytes 3145732
  218.3 20.0 %copy-start.2 = (bf16[1,4096,128]{2,1,0:T(8,128)(2,1)S(1)}, bf16[1,4096,128]{2,1,0:T(8,128)(2,1)}, u32[]{:S(2)}) copy-start(bf16[1,4096,128]{2,1,0:T(8,128)(2,1)} %param.11) | copy-start | bytes 3145732
  218.3 22.1 %copy-start.1 = (bf16[1,4096,128]{2,1,0:T(8,128)(2,1)S(1)}, bf16[1,4096,128]{2,1,0:T(8,128)(2,1)}, u32[]{:S(2)}) copy-start(bf16[1,4096,128]{2,1,0:T(8,128)(2,1)} %param.10) | copy-start | bytes 3145732
  218.3 221.3 %all-to-all-start = ((bf16[32,1,32,4096]{3,2,1,0:T(8,128)(2,1)}), bf16[32,1,32,4096]{3,2,1,0:T(8,128)(2,1)}, u32[]{:S(2)}, u32[]{:S(2)}) async-start(bf16[32,1,32,4096]{3,2,1,0:T(8,128)(2,1)} %bitcast.58), calls=%async_computation | async-start | bytes 16777216 | tf_op jit(solution)/shard_map/all_to_all | solution.py:72
  235.0 218.4 %all-gather.2.cloned.1.call-start = ((), (), s32[]{:S(2)}) async-start(), calls=%async_computation.3 | async-start | bytes 4325376 | tf_op jit(solution)/shard_map/all_gather | solution.py:83
  236.0 6.7 %collective-permute-start.1 = (bf16[4096,128]{1,0:T(8,128)(2,1)S(1)}, bf16[4096,128]{1,0:T(8,128)(2,1)}, u32[]{:S(2)}, u32[]{:S(2)}) collective-permute-start(bf16[4096,128]{1,0:T(8,128)(2,1)S(1)} %bitcast.60), channel_id=1, source_target_pairs={{0,1},{1,0},{2,3},{3,2},{4,5},{5,4},{6,7},{7,6},{8,9},{9,8},{10,11... | collective-permute-start | bytes 3145736 | tf_op jit(solution)/shard_map/ppermute | solution.py:17
  238.3 7.0 %collective-permute-start = (bf16[4096,128]{1,0:T(8,128)(2,1)S(1)}, bf16[4096,128]{1,0:T(8,128)(2,1)}, u32[]{:S(2)}, u32[]{:S(2)}) collective-permute-start(bf16[4096,128]{1,0:T(8,128)(2,1)S(1)} %bitcast.62), channel_id=1, source_target_pairs={{0,1},{1,0},{2,3},{3,2},{4,5},{5,4},{6,7},{7,6},{8,9},{9,8},{10,11... | collective-permute-start | bytes 3145736 | tf_op jit(solution)/shard_map/ppermute | solution.py:17
  240.4 5.0 %collective-permute-start.2 = (bf16[4096,128]{1,0:T(8,128)(2,1)S(1)}, bf16[4096,128]{1,0:T(8,128)(2,1)}, u32[]{:S(2)}, u32[]{:S(2)}) collective-permute-start(bf16[4096,128]{1,0:T(8,128)(2,1)S(1)} %bitcast.61), channel_id=1, source_target_pairs={{0,1},{1,0},{2,3},{3,2},{4,5},{5,4},{6,7},{7,6},{8,9},{9,8},{10,11... | collective-permute-start | bytes 3145736 | tf_op jit(solution)/shard_map/ppermute | solution.py:17
  439.6 7.1 %copy-start.4 = (bf16[4096,128]{1,0:T(8,128)(2,1)S(1)}, bf16[4096,128]{1,0:T(8,128)(2,1)}, u32[]{:S(2)}) copy-start(bf16[4096,128]{1,0:T(8,128)(2,1)} %get-tuple-element.17) | copy-start | bytes 3145732
  446.8 6.6 %copy-start.3 = (bf16[4096,128]{1,0:T(8,128)(2,1)S(1)}, bf16[4096,128]{1,0:T(8,128)(2,1)}, u32[]{:S(2)}) copy-start(bf16[4096,128]{1,0:T(8,128)(2,1)} %get-tuple-element.8) | copy-start | bytes 3145732
  459.8 8.4 %collective-permute-start.4 = (f32[512,1,256]{0,2,1:T(8,128)S(1)}, f32[512,1,256]{0,2,1:T(8,128)S(1)}, u32[]{:S(2)}, u32[]{:S(2)}) collective-permute-start(f32[512,1,256]{0,2,1:T(8,128)S(1)} %convolution_bitcast_fusion), channel_id=1, source_target_pairs={{0,1},{1,0},{2,3},{3,2},{4,5},{5,4},{6,7},{7,6},{8,9},{9,8},{10,11... | collective-permute-start | bytes 1572872 | tf_op jit(solution)/shard_map/ppermute | solution.py:17
  463.1 4.3 collective-permute-start.5
  465.0 3.2 collective-permute-start.3
Sparse Core Ops, SparseCore 0:
  11.1 201.7 all-reduce.1
Sparse Core Ops, SparseCore 1:
  237.8 125.9 all-gather.1
where the time goes:
time: 493 us
  waiting for transfers between devices  395 us (80%)
  starting transfers between devices  30.4 us (6%)
  matrix products  20.1 us (4%)
  blocking collectives  16 us (3%)
  between operations  15 us (3%)
  other arithmetic  9.41 us (2%)
  local copies, waits for them, and re-layouts  6.15 us (1%)
    psum x1, waiting for transfers between devices, broadcast(): return lax.psum(jnp.where(mine, value, jnp.zeros_like(value)), axis)  204 us
    all_to_all x1, waiting for transfers between devices, local(): lax.all_to_all(outgoing_rows, 'seq', split_axis=0, concat_axis=1, tiled=T...  191 us
    all_to_all x1, starting transfers between devices, local(): lax.all_to_all(outgoing_rows, 'seq', split_axis=0, concat_axis=1, tiled=T...  16.7 us
    all_to_all x1, blocking collectives, local(): lax.all_to_all(outgoing, 'seq', split_axis=0, concat_axis=2, tiled=True)  16 us
    ppermute x6, starting transfers between devices, partner(): return lax.ppermute(value, axis, pairs)  13.7 us
  transfers between devices with their start and end apart: 9, of which 3 were waited for; matrix products, arithmetic and copies ran while one was open for 4% of the time, Pallas kernels for 0%

commit v1 on v0

v1 whole, which is shorter than its diff:
```python
import functools

import jax
import jax.numpy as jnp
import numpy as np
from jax import lax
from jax.experimental import pallas as pl
from jax.experimental.pallas import tpu as pltpu
from jax.sharding import Mesh, PartitionSpec as P

HD = 256
AXES = ("x", "zh", "zl", "y", "core")
SIZES = (4, 4, 4, 4, 2)
SECTION = ("x", "zh")
SEQ = ("zl", "y", "core")


def pairs_of(target):
    pairs = []
    for source in range(int(np.prod(SIZES))):
        place = target(*(int(v) for v in np.unravel_index(source, SIZES)))
        if place is not None:
            pairs.append((source, int(np.ravel_multi_index(place, SIZES))))
    return pairs


def shift(dx, dy, dz):
    def target(x, zh, zl, y, core):
        sign = -1 if core else 1
        z = (zh * 4 + zl + sign * dz) % 16
        return ((x + sign * dx) % 4, z // 4, z % 4, (y + sign * dy) % 4, core)

    return pairs_of(target)


def send(value, pairs):
    return lax.ppermute(value, AXES, pairs)


def scatter_x(block):
    x = lax.axis_index("x")
    rows = block.shape[0] // 4
    quarters = [block[i * rows : (i + 1) * rows] for i in range(4)]
    got = quarters[0]
    for i in (2, 1, 3):
        pairs = pairs_of(lambda cx, zh, zl, y, c: (i, zh, zl, y, c) if cx == 0 and zh == 0 else None)
        got = jnp.where(x == i, send(quarters[i], pairs), got)
    return got


def spread_z(piece):
    zh = lax.axis_index("zh")
    core = lax.axis_index("core")
    first = pairs_of(
        lambda x, h, zl, y, c: (x, 3 if c else 1, zl, y, c) if h == 0 else None
    )

    def second_target(x, h, zl, y, c):
        near, far = (3, 1) if c else (1, 3)
        if h == 0:
            return (x, far, zl, y, c)
        if h == near:
            return (x, 2, zl, y, c)
        return None

    near = jnp.where(core == 0, 1, 3)
    piece = jnp.where(zh == near, send(piece, first), piece)
    late = send(piece, pairs_of(second_target))
    return jnp.where((zh == 0) | (zh == near), piece, late)


def widen(block, moves):
    return [block] + [send(block, shift(*move)) for move in moves]


def attend_kernel(scale, query_ref, *refs):
    *kv_refs, own_ref, send_ref = refs
    query = query_ref[...]
    scores = []
    for kv in kv_refs:
        scores.append(
            lax.dot_general(
                query, kv[:, :HD], (((1,), (1,)), ((), ())), preferred_element_type=jnp.float32
            )
            * scale
        )
    top = functools.reduce(jnp.maximum, [jnp.max(s, axis=-1, keepdims=True) for s in scores])
    denom = jnp.zeros_like(top)
    numer = jnp.zeros((query.shape[0], HD), jnp.float32)
    for kv, s in zip(kv_refs, scores):
        probs = jnp.exp(s - top).astype(jnp.bfloat16)
        denom += jnp.sum(probs.astype(jnp.float32), axis=-1, keepdims=True)
        numer += jnp.dot(probs, kv[:, HD:], preferred_element_type=jnp.float32)
    half = HD // 2
    lane = lax.broadcasted_iota(jnp.int32, (query.shape[0], half), 1)
    stats = jnp.where(lane < half // 2, top, denom)
    own_ref[:, :half] = numer[:, :half]
    own_ref[:, half:] = stats
    send_ref[:, :half] = numer[:, half:]
    send_ref[:, half:] = stats


def attend(queries, key_values):
    count = queries.shape[0]
    block = 128
    out = jax.ShapeDtypeStruct((count, HD), jnp.float32)
    row_spec = pl.BlockSpec((block, HD), lambda i: (i, 0))
    keys = sum(kv.shape[0] for kv in key_values)
    return pl.pallas_call(
        functools.partial(attend_kernel, HD**-0.5),
        out_shape=(out, out),
        grid=(count // block,),
        in_specs=[row_spec] + [pl.BlockSpec(kv.shape, lambda i: (0, 0)) for kv in key_values],
        out_specs=(row_spec, row_spec),
        compiler_params=pltpu.CompilerParams(vmem_limit_bytes=40 * 2**20),
        cost_estimate=pl.CostEstimate(
            flops=4 * count * keys * HD,
            bytes_accessed=keys * HD * 4 + count * HD * 10,
            transcendentals=count * keys,
        ),
    )(queries, *key_values)


def local(section_states, dec_states, norm_gain, w_query, w_key, w_value):
    model_width = dec_states.shape[2]
    dec_count = dec_states.shape[1]
    seq_count = lax.axis_size(SEQ)
    half = HD // 2

    states = dec_states[0].astype(jnp.float32)
    mean_square = jnp.mean(states * states, axis=-1, keepdims=True)
    normed = (states * lax.rsqrt(mean_square + 1e-06) * norm_gain[0]).astype(jnp.bfloat16)
    normed_all = lax.all_gather(normed, SEQ, axis=0, tiled=True)

    other_core = pairs_of(lambda x, zh, zl, y, c: (x, zh, zl, y, 1 - c))
    mine = (w_key[0], w_value[0], w_query[0])
    other = [send(w, other_core) for w in mine]

    piece = spread_z(scatter_x(section_states[0]))
    piece = jnp.concatenate(widen(piece, ((2, 2, 2), (1, 1, -1), (-1, -1, 1))), axis=0)
    quarter = jnp.concatenate(widen(piece, ((1, 0, 1), (-1, 0, -1), (0, 2, 0))), axis=0)
    one_hop = ((1, 0, 0), (0, 1, 0), (0, 0, 1))
    middle = quarter.shape[0] // 2
    first = widen(quarter[:middle], one_hop)
    second = widen(quarter[middle:], one_hop)
    blocks = [quarter] + first[1:] + second[1:]

    kv_cols = jnp.concatenate([mine[0], other[0], mine[1], other[1]], axis=1)
    query_cols = jnp.concatenate([mine[2], other[2]], axis=1)
    queries = jnp.dot(normed_all, query_cols, preferred_element_type=jnp.float32).astype(jnp.bfloat16)
    key_values = [
        jnp.dot(rows, kv_cols, preferred_element_type=jnp.float32).astype(jnp.bfloat16) for rows in blocks
    ]

    own, outgoing = attend(queries, key_values)
    arrived = send(outgoing, other_core)
    stat = lambda a: (a[:, half : half + 1], a[:, half + half // 2 : half + half // 2 + 1])
    (top_a, denom_a), (top_b, denom_b) = stat(own), stat(arrived)
    joint = jnp.maximum(top_a, top_b)
    factor_a, factor_b = jnp.exp(top_a - joint), jnp.exp(top_b - joint)
    numer = own[:, :half] * factor_a + arrived[:, :half] * factor_b
    merged = (numer / (denom_a * factor_a + denom_b * factor_b)).astype(jnp.bfloat16)

    parts = merged.reshape(seq_count, dec_count, half)
    returned = lax.all_to_all(parts, SEQ, split_axis=0, concat_axis=0, tiled=True)
    return jnp.transpose(returned, (1, 0, 2)).reshape(1, dec_count, model_width)


def solution(mesh):
    fine = Mesh(mesh.devices.reshape(SIZES), AXES)
    in_specs = (
        P(SECTION, SEQ, None),
        P(SECTION, SEQ, None),
        P(SECTION, None),
        P(SECTION, None, SEQ),
        P(SECTION, None, SEQ),
        P(SECTION, None, SEQ),
    )
    return jax.shard_map(
        local, mesh=fine, in_specs=in_specs, out_specs=P(SECTION, SEQ, None), check_vma=False
    )
```

time: 493 us -> 173 us (0.35)
  waiting for transfers between devices: 395 us -> 51.2 us
  starting transfers between devices: 30.4 us -> 76.3 us
  matrix products: 20.1 us -> 9.29 us
    psum x1 -> x0, waiting for transfers between devices: 204 us -> none  [broadcast(): return lax.psum(jnp.where(mine, value, jnp.zeros_like(value)), axis)]
    all_to_all x1 -> x0, waiting for transfers between devices: 191 us -> none  [local(): lax.all_to_all(outgoing_rows, 'seq', split_axis=0, concat_axis=1, tiled=T...]
    ppermute x6 -> x21, starting transfers between devices: 13.7 us -> 76.3 us  [send(): return lax.ppermute(value, AXES, pairs)]
    ppermute x6 -> x21, waiting for transfers between devices: 0.79 us -> 51.2 us  [send(): return lax.ppermute(value, AXES, pairs)]
    all_to_all x1 -> x0, starting transfers between devices: 16.7 us -> none  [local(): lax.all_to_all(outgoing_rows, 'seq', split_axis=0, concat_axis=1, tiled=T...]
    dot_general x4 -> x8, matrix products: 20.1 us -> 9.29 us  [the longest x7 5.55 us: local(): jnp.dot(rows, kv_cols, preferred_element_type=jnp.float32)]
    select_n x3 -> x2, other arithmetic: 7.93 us -> 0.94 us  [the longest x1 0.93 us: scatter_x(): got = jnp.where(x == i, send(quarters[i], pairs), got)]
    another operation x1 -> x0, local copies, waits for them, and re-layouts: 5.34 us -> none  [local(): outgoing_rows = jnp.tile(row_halves, (group_count, 1, 1))[:, None]]
  transfers between devices with their start and end apart: 9 -> 22, of which waited for: 3 -> 10; matrix products, arithmetic and copies ran while one was open for 4% -> 5% of each run, Pallas kernels for 0% -> 0%
where the time goes in v1:
time: 173 us
  starting transfers between devices  76.3 us (44%)
  waiting for transfers between devices  51.2 us (30%)
  between operations  13.9 us (8%)
  blocking collectives  11.7 us (7%)
  matrix products  9.29 us (5%)
  other arithmetic  4.98 us (3%)
  Pallas kernels  3.19 us (2%)
  local copies, waits for them, and re-layouts  2.18 us (1%)
    ppermute x21, starting transfers between devices, send(): return lax.ppermute(value, AXES, pairs)  76.3 us
    ppermute x21, waiting for transfers between devices, send(): return lax.ppermute(value, AXES, pairs)  51.2 us
    all_to_all x1, blocking collectives, local(): lax.all_to_all(parts, SEQ, split_axis=0, concat_axis=0, tiled=True)  11.7 us
    dot_general x7, matrix products, local(): jnp.dot(rows, kv_cols, preferred_element_type=jnp.float32)  5.55 us
    dot_general x1, matrix products, local(): jnp.dot(normed_all, query_cols, preferred_element_type=jnp.float32)  3.73 us
  transfers between devices with their start and end apart: 22, of which 10 were waited for; matrix products, arithmetic and copies ran while one was open for 5% of the time, Pallas kernels for 0%

profile of v1, /device:TPU:1, one launch (start us, length us, event | category | flops | bytes accessed | tf_op | source)
XLA Modules:
  0.0 172.7 jit_solution(9237228986447267100)
XLA Ops:
  6.5 1.1 slice_bitcast_fusion
  7.6 5.2 %collective-permute-start.1 = (bf16[16,4096]{1,0:T(8,128)(2,1)S(1)}, bf16[16,4096]{1,0:T(8,128)(2,1)S(1)}, u32[]{:S(2)}, u32[]{:S(2)}) collective-permute-start(bf16[16,4096]{1,0:T(8,128)(2,1)S(1)} %get-tuple-element.22), channel_id=1, source_target_pairs={{0,384},{1,385},{2,386},{3,387},{4,388},{5,389},{6,390},{7,391},{8... | collective-permute-start | bytes 393224 | tf_op jit(solution)/shard_map/ppermute | solution.py:37
  12.8 1.3 collective-permute-start.2
  14.1 1.3 collective-permute-start.3
  15.4 1.1 fusion.7
  16.5 0.0 collective-permute-done.1
  16.5 0.0 collective-permute-done.2
  16.5 0.9 collective-permute-done.3
  17.4 0.9 fusion.18
  18.4 6.6 %collective-permute-start.4 = (bf16[16,4096]{1,0:T(8,128)(2,1)S(1)}, bf16[16,4096]{1,0:T(8,128)(2,1)S(1)}, u32[]{:S(2)}, u32[]{:S(2)}) collective-permute-start(bf16[16,4096]{1,0:T(8,128)(2,1)S(1)} %fusion.18), channel_id=1, source_target_pairs={{0,32},{1,97},{2,34},{3,99},{4,36},{5,101},{6,38},{7,103},{8,40},{... | collective-permute-start | bytes 393224 | tf_op jit(solution)/shard_map/ppermute | solution.py:37
  25.0 1.7 fusion.9
  26.6 0.0 all-gather.2.cloned.1.call-update
  26.7 7.9 %collective-permute-done.4 = bf16[16,4096]{1,0:T(8,128)(2,1)S(1)} collective-permute-done((bf16[16,4096]{1,0:T(8,128)(2,1)S(1)}, bf16[16,4096]{1,0:T(8,128)(2,1)S(1)}, u32[]{:S(2)}, u32[]{:S(2)}) %collective-permute-start.4) | collective-permute-done | bytes 131104 | tf_op jit(solution)/shard_map/ppermute | solution.py:37
  34.6 1.3 collective-permute-start.5
  35.9 1.9 %collective-permute-start = (bf16[4096,128]{1,0:T(8,128)(2,1)}, bf16[4096,128]{1,0:T(8,128)(2,1)}, u32[]{:S(2)}, u32[]{:S(2)}) collective-permute-start(bf16[4096,128]{1,0:T(8,128)(2,1)} %bitcast.44), channel_id=1, source_target_pairs={{0,1},{1,0},{2,3},{3,2},{4,5},{5,4},{6,7},{7,6},{8,9},{9,8},{10,11... | collective-permute-start | bytes 3145736 | tf_op jit(solution)/shard_map/ppermute | solution.py:37
  37.8 2.4 %collective-permute-start.13 = (bf16[4096,128]{1,0:T(8,128)(2,1)}, bf16[4096,128]{1,0:T(8,128)(2,1)S(1)}, u32[]{:S(2)}, u32[]{:S(2)}) collective-permute-start(bf16[4096,128]{1,0:T(8,128)(2,1)} %bitcast.37), channel_id=1, source_target_pairs={{0,1},{1,0},{2,3},{3,2},{4,5},{5,4},{6,7},{7,6},{8,9},{9,8},{10,11... | collective-permute-start | bytes 3145736 | tf_op jit(solution)/shard_map/ppermute | solution.py:37
  40.2 0.0 collective-permute-done.5
  40.3 2.1 %collective-permute-start.8 = (bf16[16,4096]{1,0:T(8,128)(2,1)S(1)}, bf16[16,4096]{1,0:T(8,128)(2,1)S(1)}, u32[]{:S(2)}, u32[]{:S(2)}) collective-permute-start(bf16[16,4096]{1,0:T(8,128)(2,1)S(1)} %get-tuple-element.13), channel_id=1, source_target_pairs={{0,398},{1,251},{2,392},{3,253},{4,394},{5,255},{6,396},{7,249},{8... | collective-permute-start | bytes 393224 | tf_op jit(solution)/shard_map/ppermute | solution.py:37
  42.4 7.4 %collective-permute-start.7 = (bf16[16,4096]{1,0:T(8,128)(2,1)S(1)}, bf16[16,4096]{1,0:T(8,128)(2,1)S(1)}, u32[]{:S(2)}, u32[]{:S(2)}) collective-permute-start(bf16[16,4096]{1,0:T(8,128)(2,1)S(1)} %get-tuple-element.13), channel_id=1, source_target_pairs={{0,250},{1,399},{2,252},{3,393},{4,254},{5,395},{6,248},{7,397},{8... | collective-permute-start | bytes 393224 | tf_op jit(solution)/shard_map/ppermute | solution.py:37
  49.8 5.3 %collective-permute-start.6 = (bf16[16,4096]{1,0:T(8,128)(2,1)S(1)}, bf16[16,4096]{1,0:T(8,128)(2,1)S(1)}, u32[]{:S(2)}, u32[]{:S(2)}) collective-permute-start(bf16[16,4096]{1,0:T(8,128)(2,1)S(1)} %get-tuple-element.13), channel_id=1, source_target_pairs={{0,276},{1,373},{2,278},{3,375},{4,272},{5,369},{6,274},{7,371},{8... | collective-permute-start | bytes 393224 | tf_op jit(solution)/shard_map/ppermute | solution.py:37
  55.1 1.9 %collective-permute-start.12 = (bf16[4096,128]{1,0:T(8,128)(2,1)}, bf16[4096,128]{1,0:T(8,128)(2,1)S(1)}, u32[]{:S(2)}, u32[]{:S(2)}) collective-permute-start(bf16[4096,128]{1,0:T(8,128)(2,1)} %bitcast.39), channel_id=1, source_target_pairs={{0,1},{1,0},{2,3},{3,2},{4,5},{5,4},{6,7},{7,6},{8,9},{9,8},{10,11... | collective-permute-start | bytes 3145736 | tf_op jit(solution)/shard_map/ppermute | solution.py:37
  57.0 0.0 collective-permute-done.7
  57.0 6.1 %collective-permute-done.6 = bf16[16,4096]{1,0:T(8,128)(2,1)S(1)} collective-permute-done((bf16[16,4096]{1,0:T(8,128)(2,1)S(1)}, bf16[16,4096]{1,0:T(8,128)(2,1)S(1)}, u32[]{:S(2)}, u32[]{:S(2)}) %collective-permute-start.6) | collective-permute-done | bytes 131104 | tf_op jit(solution)/shard_map/ppermute | solution.py:37
  63.2 1.9 %collective-permute-start.10 = (bf16[64,4096]{1,0:T(8,128)(2,1)S(1)}, bf16[64,4096]{1,0:T(8,128)(2,1)S(1)}, u32[]{:S(2)}, u32[]{:S(2)}) collective-permute-start(bf16[64,4096]{1,0:T(8,128)(2,1)S(1)} %pad_maximum_fusion.1), channel_id=1, source_target_pairs={{0,504},{1,137},{2,506},{3,139},{4,508},{5,141},{6,510},{7,143},{8... | collective-permute-start | bytes 1572872 | tf_op jit(solution)/shard_map/ppermute | solution.py:37
  65.1 6.7 %collective-permute-start.9 = (bf16[64,4096]{1,0:T(8,128)(2,1)S(1)}, bf16[64,4096]{1,0:T(8,128)(2,1)S(1)}, u32[]{:S(2)}, u32[]{:S(2)}) collective-permute-start(bf16[64,4096]{1,0:T(8,128)(2,1)S(1)} %pad_maximum_fusion.1), channel_id=1, source_target_pairs={{0,136},{1,505},{2,138},{3,507},{4,140},{5,509},{6,142},{7,511},{8... | collective-permute-start | bytes 1572872 | tf_op jit(solution)/shard_map/ppermute | solution.py:37
  71.9 17.0 %collective-permute-done.9 = bf16[64,4096]{1,0:T(8,128)(2,1)S(1)} collective-permute-done((bf16[64,4096]{1,0:T(8,128)(2,1)S(1)}, bf16[64,4096]{1,0:T(8,128)(2,1)S(1)}, u32[]{:S(2)}, u32[]{:S(2)}) %collective-permute-start.9) | collective-permute-done | bytes 524320 | tf_op jit(solution)/shard_map/ppermute | solution.py:37
  88.9 1.9 %collective-permute-start.11 = (bf16[64,4096]{1,0:T(8,128)(2,1)S(1)}, bf16[64,4096]{1,0:T(8,128)(2,1)S(1)}, u32[]{:S(2)}, u32[]{:S(2)}) collective-permute-start(bf16[64,4096]{1,0:T(8,128)(2,1)S(1)} %pad_maximum_fusion.1), channel_id=1, source_target_pairs={{0,4},{1,5},{2,6},{3,7},{4,0},{5,1},{6,2},{7,3},{8,12},{9,13},{10,... | collective-permute-start | bytes 1572872 | tf_op jit(solution)/shard_map/ppermute | solution.py:37
  90.8 0.1 constant_dynamic-update-slice_fusion.7
  90.9 0.0 collective-permute-done.10
  90.9 4.6 %collective-permute-start.14 = (bf16[128,4096]{1,0:T(8,128)(2,1)S(1)}, bf16[128,4096]{1,0:T(8,128)(2,1)S(1)}, u32[]{:S(2)}, u32[]{:S(2)}) collective-permute-start(bf16[128,4096]{1,0:T(8,128)(2,1)S(1)} %get-tuple-element.18), channel_id=1, source_target_pairs={{0,128},{1,385},{2,130},{3,387},{4,132},{5,389},{6,134},{7,391},{8... | collective-permute-start | bytes 3145736 | tf_op jit(solution)/shard_map/ppermute | solution.py:37
  95.5 0.1 constant_dynamic-update-slice_fusion.13
  95.6 7.8 %collective-permute-done.11 = bf16[64,4096]{1,0:T(8,128)(2,1)S(1)} collective-permute-done((bf16[64,4096]{1,0:T(8,128)(2,1)S(1)}, bf16[64,4096]{1,0:T(8,128)(2,1)S(1)}, u32[]{:S(2)}, u32[]{:S(2)}) %collective-permute-start.11) | collective-permute-done | bytes 524320 | tf_op jit(solution)/shard_map/ppermute | solution.py:37
  103.4 3.6 %collective-permute-start.15 = (bf16[128,4096]{1,0:T(8,128)(2,1)S(1)}, bf16[128,4096]{1,0:T(8,128)(2,1)S(1)}, u32[]{:S(2)}, u32[]{:S(2)}) collective-permute-start(bf16[128,4096]{1,0:T(8,128)(2,1)S(1)} %get-tuple-element.18), channel_id=1, source_target_pairs={{0,2},{1,7},{2,4},{3,1},{4,6},{5,3},{6,0},{7,5},{8,10},{9,15},{10,... | collective-permute-start | bytes 3145736 | tf_op jit(solution)/shard_map/ppermute | solution.py:37
  107.0 0.1 constant_dynamic-update-slice_fusion.12
  107.2 0.0 collective-permute-done.13
  107.2 3.9 %collective-permute-start.16 = (bf16[128,4096]{1,0:T(8,128)(2,1)S(1)}, bf16[128,4096]{1,0:T(8,128)(2,1)S(1)}, u32[]{:S(2)}, u32[]{:S(2)}) collective-permute-start(bf16[128,4096]{1,0:T(8,128)(2,1)S(1)} %get-tuple-element.18), channel_id=1, source_target_pairs={{0,8},{1,121},{2,10},{3,123},{4,12},{5,125},{6,14},{7,127},{8,16},... | collective-permute-start | bytes 3145736 | tf_op jit(solution)/shard_map/ppermute | solution.py:37
  111.1 0.0 collective-permute-done.12
  111.1 3.2 %collective-permute-start.17 = (bf16[128,4096]{1,0:T(8,128)(2,1)S(1)}, bf16[128,4096]{1,0:T(8,128)(2,1)S(1)}, u32[]{:S(2)}, u32[]{:S(2)}) collective-permute-start(bf16[128,4096]{1,0:T(8,128)(2,1)S(1)} %get-tuple-element.14), channel_id=1, source_target_pairs={{0,128},{1,385},{2,130},{3,387},{4,132},{5,389},{6,134},{7,391},{8... | collective-permute-start | bytes 3145736 | tf_op jit(solution)/shard_map/ppermute | solution.py:37
  114.3 0.5 pad_maximum_fusion
  114.8 1.2 convolution_convert_fusion.refs_0_
  116.0 0.0 collective-permute-done.14
  116.0 1.9 %collective-permute-start.18 = (bf16[128,4096]{1,0:T(8,128)(2,1)S(1)}, bf16[128,4096]{1,0:T(8,128)(2,1)S(1)}, u32[]{:S(2)}, u32[]{:S(2)}) collective-permute-start(bf16[128,4096]{1,0:T(8,128)(2,1)S(1)} %get-tuple-element.14), channel_id=1, source_target_pairs={{0,2},{1,7},{2,4},{3,1},{4,6},{5,3},{6,0},{7,5},{8,10},{9,15},{10,... | collective-permute-start | bytes 3145736 | tf_op jit(solution)/shard_map/ppermute | solution.py:37
  118.0 0.7 convolution_convert_fusion.6.refs_1_
  118.7 0.5 collective-permute-done.15
  119.2 4.8 %collective-permute-start.19 = (bf16[128,4096]{1,0:T(8,128)(2,1)S(1)}, bf16[128,4096]{1,0:T(8,128)(2,1)S(1)}, u32[]{:S(2)}, u32[]{:S(2)}) collective-permute-start(bf16[128,4096]{1,0:T(8,128)(2,1)S(1)} %get-tuple-element.14), channel_id=1, source_target_pairs={{0,8},{1,121},{2,10},{3,123},{4,12},{5,125},{6,14},{7,127},{8,16},... | collective-permute-start | bytes 3145736 | tf_op jit(solution)/shard_map/ppermute | solution.py:37
  124.1 0.7 convolution_convert_fusion.5.refs_2_
  124.8 0.7 convolution_convert_fusion.4.refs_3_
  125.5 1.4 collective-permute-done.17
  126.9 0.7 convolution_convert_fusion.3.refs_4_
  127.6 0.0 copy-start.2
  127.7 4.2 %collective-permute-done.18 = bf16[128,4096]{1,0:T(8,128)(2,1)S(1)} collective-permute-done((bf16[128,4096]{1,0:T(8,128)(2,1)S(1)}, bf16[128,4096]{1,0:T(8,128)(2,1)S(1)}, u32[]{:S(2)}, u32[]{:S(2)}) %collective-permute-start.18) | collective-permute-done | bytes 1048608 | tf_op jit(solution)/shard_map/ppermute | solution.py:37
  131.9 0.7 convolution_convert_fusion.2.refs_5_
  132.6 3.9 %collective-permute-done.19 = bf16[128,4096]{1,0:T(8,128)(2,1)S(1)} collective-permute-done((bf16[128,4096]{1,0:T(8,128)(2,1)S(1)}, bf16[128,4096]{1,0:T(8,128)(2,1)S(1)}, u32[]{:S(2)}, u32[]{:S(2)}) %collective-permute-start.19) | collective-permute-done | bytes 1048608 | tf_op jit(solution)/shard_map/ppermute | solution.py:37
  136.5 0.7 convolution_convert_fusion.1.refs_6_
  137.2 0.0 collective-permute-done
  137.2 0.0 all-gather.2.cloned.1.call-done
  137.3 3.7 %fusion.4.query_ref = bf16[512,256]{1,0:T(8,128)(2,1)S(1)} fusion(bf16[512,4096]{1,0:T(8,128)(2,1)} %all-gather.2.cloned.1.call-done, bf16[4096,128]{1,0:T(8,128)(2,1)} %collective-permute-done, bf16[4096,128]{1,0:T(8,128)(2,1)S(1)} %bitcast.45), kind=kOutput, calls=%fused_computation.5 | convolution fusion | flops 1078067200 | bytes 6553600 | tf_op jit(solution)/shard_map/dot_general | solution.py:150
  141.0 3.2 %shard_map.64 = (f32[512,256]{1,0:T(8,128)S(1)}, f32[512,256]{1,0:T(8,128)S(1)}) custom-call(bf16[512,256]{1,0:T(8,128)(2,1)S(1)} %fusion.4.query_ref, bf16[256,512]{1,0:T(8,128)(2,1)S(1)} %convolution_convert_fusion.refs_0_, bf16[128,512]{1,0:T(8,128)(2,1)S(1)} %convolution_convert_fusion.6.refs_1_, bf16[128,512]{1,0:T(8,128)(2,1)S(1)} %convolution_convert_fusion.5.refs_2_, ...), custom_call_target="tpu_custom_call" | custom-call | flops 536870912 | bytes 2359296 | tf_op jit(solution)/shard_map/pallas_call | solution.py:109
  144.2 6.9 %collective-permute-start.20 = (f32[512,256]{1,0:T(8,128)S(1)}, f32[512,256]{1,0:T(8,128)S(1)}, u32[]{:S(2)}, u32[]{:S(2)}) collective-permute-start(f32[512,256]{1,0:T(8,128)S(1)} %get-tuple-element.8), channel_id=1, source_target_pairs={{0,1},{1,0},{2,3},{3,2},{4,5},{5,4},{6,7},{7,6},{8,9},{9,8},{10,11... | collective-permute-start | bytes 1572872 | tf_op jit(solution)/shard_map/ppermute | solution.py:37
  151.1 1.5 collective-permute-done.20
  152.7 0.5 fusion.20
  153.1 0.3 fusion.16
  153.4 11.7 %all_to_all.5 = bf16[32,16,128]{2,1,0:T(8,128)(2,1)S(1)} all-to-all(bf16[32,16,128]{2,1,0:T(8,128)(2,1)S(1)} %bitcast.41), channel_id=1, replica_groups=mesh['x'=4,'zh'=4,'zl'=4,'y'=4,'core'=2] {'zl','y','core'}, dimensions={0} | all-to-all | bytes 262144 | tf_op jit(solution)/shard_map/all_to_all | solution.py:165
  165.1 0.7 reshape.21
  (17 shorter events, 0.2 us)
Async XLA Ops:
  6.5 130.7 %all-gather.2.cloned.1.call-start = ((), (), s32[]{:S(2)}) async-start(), calls=%async_computation.1 | async-start | bytes 4325376 | tf_op jit(solution)/shard_map/all_gather | solution.py:133
  7.6 8.9 %collective-permute-start.1 = (bf16[16,4096]{1,0:T(8,128)(2,1)S(1)}, bf16[16,4096]{1,0:T(8,128)(2,1)S(1)}, u32[]{:S(2)}, u32[]{:S(2)}) collective-permute-start(bf16[16,4096]{1,0:T(8,128)(2,1)S(1)} %get-tuple-element.22), channel_id=1, source_target_pairs={{0,384},{1,385},{2,386},{3,387},{4,388},{5,389},{6,390},{7,391},{8... | collective-permute-start | bytes 393224 | tf_op jit(solution)/shard_map/ppermute | solution.py:37
  12.8 3.7 %collective-permute-start.2 = (bf16[16,4096]{1,0:T(8,128)(2,1)S(1)}, bf16[16,4096]{1,0:T(8,128)(2,1)S(1)}, u32[]{:S(2)}, u32[]{:S(2)}) collective-permute-start(bf16[16,4096]{1,0:T(8,128)(2,1)S(1)} %get-tuple-element.21), channel_id=1, source_target_pairs={{0,128},{1,129},{2,130},{3,131},{4,132},{5,133},{6,134},{7,135},{8... | collective-permute-start | bytes 393224 | tf_op jit(solution)/shard_map/ppermute | solution.py:37
  14.1 3.3 %collective-permute-start.3 = (bf16[16,4096]{1,0:T(8,128)(2,1)S(1)}, bf16[16,4096]{1,0:T(8,128)(2,1)S(1)}, u32[]{:S(2)}, u32[]{:S(2)}) collective-permute-start(bf16[16,4096]{1,0:T(8,128)(2,1)S(1)} %get-tuple-element.20), channel_id=1, source_target_pairs={{0,256},{1,257},{2,258},{3,259},{4,260},{5,261},{6,262},{7,263},{8... | collective-permute-start | bytes 393224 | tf_op jit(solution)/shard_map/ppermute | solution.py:37
  18.4 16.2 %collective-permute-start.4 = (bf16[16,4096]{1,0:T(8,128)(2,1)S(1)}, bf16[16,4096]{1,0:T(8,128)(2,1)S(1)}, u32[]{:S(2)}, u32[]{:S(2)}) collective-permute-start(bf16[16,4096]{1,0:T(8,128)(2,1)S(1)} %fusion.18), channel_id=1, source_target_pairs={{0,32},{1,97},{2,34},{3,99},{4,36},{5,101},{6,38},{7,103},{8,40},{... | collective-permute-start | bytes 393224 | tf_op jit(solution)/shard_map/ppermute | solution.py:37
  26.6 87.6 %copy-start = (bf16[1,4096,128]{2,1,0:T(8,128)(2,1)S(1)}, bf16[1,4096,128]{2,1,0:T(8,128)(2,1)}, u32[]{:S(2)}) copy-start(bf16[1,4096,128]{2,1,0:T(8,128)(2,1)} %param.11) | copy-start | bytes 3145732
  26.6 87.6 %copy-start.1 = (bf16[1,4096,128]{2,1,0:T(8,128)(2,1)S(1)}, bf16[1,4096,128]{2,1,0:T(8,128)(2,1)}, u32[]{:S(2)}) copy-start(bf16[1,4096,128]{2,1,0:T(8,128)(2,1)} %param.10) | copy-start | bytes 3145732
  34.6 5.7 %collective-permute-start.5 = (bf16[16,4096]{1,0:T(8,128)(2,1)S(1)}, bf16[16,4096]{1,0:T(8,128)(2,1)S(1)}, u32[]{:S(2)}, u32[]{:S(2)}) collective-permute-start(bf16[16,4096]{1,0:T(8,128)(2,1)S(1)} %broadcast_select_fusion), channel_id=1, source_target_pairs={{0,96},{1,33},{2,98},{3,35},{4,100},{5,37},{6,102},{7,39},{8,104},... | collective-permute-start | bytes 393224 | tf_op jit(solution)/shard_map/ppermute | solution.py:37
  35.9 101.3 %collective-permute-start = (bf16[4096,128]{1,0:T(8,128)(2,1)}, bf16[4096,128]{1,0:T(8,128)(2,1)}, u32[]{:S(2)}, u32[]{:S(2)}) collective-permute-start(bf16[4096,128]{1,0:T(8,128)(2,1)} %bitcast.44), channel_id=1, source_target_pairs={{0,1},{1,0},{2,3},{3,2},{4,5},{5,4},{6,7},{7,6},{8,9},{9,8},{10,11... | collective-permute-start | bytes 3145736 | tf_op jit(solution)/shard_map/ppermute | solution.py:37
  37.8 69.3 %collective-permute-start.13 = (bf16[4096,128]{1,0:T(8,128)(2,1)}, bf16[4096,128]{1,0:T(8,128)(2,1)S(1)}, u32[]{:S(2)}, u32[]{:S(2)}) collective-permute-start(bf16[4096,128]{1,0:T(8,128)(2,1)} %bitcast.37), channel_id=1, source_target_pairs={{0,1},{1,0},{2,3},{3,2},{4,5},{5,4},{6,7},{7,6},{8,9},{9,8},{10,11... | collective-permute-start | bytes 3145736 | tf_op jit(solution)/shard_map/ppermute | solution.py:37
  40.3 14.8 %collective-permute-start.8 = (bf16[16,4096]{1,0:T(8,128)(2,1)S(1)}, bf16[16,4096]{1,0:T(8,128)(2,1)S(1)}, u32[]{:S(2)}, u32[]{:S(2)}) collective-permute-start(bf16[16,4096]{1,0:T(8,128)(2,1)S(1)} %get-tuple-element.13), channel_id=1, source_target_pairs={{0,398},{1,251},{2,392},{3,253},{4,394},{5,255},{6,396},{7,249},{8... | collective-permute-start | bytes 393224 | tf_op jit(solution)/shard_map/ppermute | solution.py:37
  42.4 14.7 %collective-permute-start.7 = (bf16[16,4096]{1,0:T(8,128)(2,1)S(1)}, bf16[16,4096]{1,0:T(8,128)(2,1)S(1)}, u32[]{:S(2)}, u32[]{:S(2)}) collective-permute-start(bf16[16,4096]{1,0:T(8,128)(2,1)S(1)} %get-tuple-element.13), channel_id=1, source_target_pairs={{0,250},{1,399},{2,252},{3,393},{4,254},{5,395},{6,248},{7,397},{8... | collective-permute-start | bytes 393224 | tf_op jit(solution)/shard_map/ppermute | solution.py:37
  49.8 13.3 %collective-permute-start.6 = (bf16[16,4096]{1,0:T(8,128)(2,1)S(1)}, bf16[16,4096]{1,0:T(8,128)(2,1)S(1)}, u32[]{:S(2)}, u32[]{:S(2)}) collective-permute-start(bf16[16,4096]{1,0:T(8,128)(2,1)S(1)} %get-tuple-element.13), channel_id=1, source_target_pairs={{0,276},{1,373},{2,278},{3,375},{4,272},{5,369},{6,274},{7,371},{8... | collective-permute-start | bytes 393224 | tf_op jit(solution)/shard_map/ppermute | solution.py:37
  55.1 56.0 %collective-permute-start.12 = (bf16[4096,128]{1,0:T(8,128)(2,1)}, bf16[4096,128]{1,0:T(8,128)(2,1)S(1)}, u32[]{:S(2)}, u32[]{:S(2)}) collective-permute-start(bf16[4096,128]{1,0:T(8,128)(2,1)} %bitcast.39), channel_id=1, source_target_pairs={{0,1},{1,0},{2,3},{3,2},{4,5},{5,4},{6,7},{7,6},{8,9},{9,8},{10,11... | collective-permute-start | bytes 3145736 | tf_op jit(solution)/shard_map/ppermute | solution.py:37
  63.2 27.7 %collective-permute-start.10 = (bf16[64,4096]{1,0:T(8,128)(2,1)S(1)}, bf16[64,4096]{1,0:T(8,128)(2,1)S(1)}, u32[]{:S(2)}, u32[]{:S(2)}) collective-permute-start(bf16[64,4096]{1,0:T(8,128)(2,1)S(1)} %pad_maximum_fusion.1), channel_id=1, source_target_pairs={{0,504},{1,137},{2,506},{3,139},{4,508},{5,141},{6,510},{7,143},{8... | collective-permute-start | bytes 1572872 | tf_op jit(solution)/shard_map/ppermute | solution.py:37
  65.1 23.8 %collective-permute-start.9 = (bf16[64,4096]{1,0:T(8,128)(2,1)S(1)}, bf16[64,4096]{1,0:T(8,128)(2,1)S(1)}, u32[]{:S(2)}, u32[]{:S(2)}) collective-permute-start(bf16[64,4096]{1,0:T(8,128)(2,1)S(1)} %pad_maximum_fusion.1), channel_id=1, source_target_pairs={{0,136},{1,505},{2,138},{3,507},{4,140},{5,509},{6,142},{7,511},{8... | collective-permute-start | bytes 1572872 | tf_op jit(solution)/shard_map/ppermute | solution.py:37
  88.9 14.5 %collective-permute-start.11 = (bf16[64,4096]{1,0:T(8,128)(2,1)S(1)}, bf16[64,4096]{1,0:T(8,128)(2,1)S(1)}, u32[]{:S(2)}, u32[]{:S(2)}) collective-permute-start(bf16[64,4096]{1,0:T(8,128)(2,1)S(1)} %pad_maximum_fusion.1), channel_id=1, source_target_pairs={{0,4},{1,5},{2,6},{3,7},{4,0},{5,1},{6,2},{7,3},{8,12},{9,13},{10,... | collective-permute-start | bytes 1572872 | tf_op jit(solution)/shard_map/ppermute | solution.py:37
  90.9 25.1 %collective-permute-start.14 = (bf16[128,4096]{1,0:T(8,128)(2,1)S(1)}, bf16[128,4096]{1,0:T(8,128)(2,1)S(1)}, u32[]{:S(2)}, u32[]{:S(2)}) collective-permute-start(bf16[128,4096]{1,0:T(8,128)(2,1)S(1)} %get-tuple-element.18), channel_id=1, source_target_pairs={{0,128},{1,385},{2,130},{3,387},{4,132},{5,389},{6,134},{7,391},{8... | collective-permute-start | bytes 3145736 | tf_op jit(solution)/shard_map/ppermute | solution.py:37
  103.4 15.8 %collective-permute-start.15 = (bf16[128,4096]{1,0:T(8,128)(2,1)S(1)}, bf16[128,4096]{1,0:T(8,128)(2,1)S(1)}, u32[]{:S(2)}, u32[]{:S(2)}) collective-permute-start(bf16[128,4096]{1,0:T(8,128)(2,1)S(1)} %get-tuple-element.18), channel_id=1, source_target_pairs={{0,2},{1,7},{2,4},{3,1},{4,6},{5,3},{6,0},{7,5},{8,10},{9,15},{10,... | collective-permute-start | bytes 3145736 | tf_op jit(solution)/shard_map/ppermute | solution.py:37
  107.2 17.6 %collective-permute-start.16 = (bf16[128,4096]{1,0:T(8,128)(2,1)S(1)}, bf16[128,4096]{1,0:T(8,128)(2,1)S(1)}, u32[]{:S(2)}, u32[]{:S(2)}) collective-permute-start(bf16[128,4096]{1,0:T(8,128)(2,1)S(1)} %get-tuple-element.18), channel_id=1, source_target_pairs={{0,8},{1,121},{2,10},{3,123},{4,12},{5,125},{6,14},{7,127},{8,16},... | collective-permute-start | bytes 3145736 | tf_op jit(solution)/shard_map/ppermute | solution.py:37
  111.1 15.8 %collective-permute-start.17 = (bf16[128,4096]{1,0:T(8,128)(2,1)S(1)}, bf16[128,4096]{1,0:T(8,128)(2,1)S(1)}, u32[]{:S(2)}, u32[]{:S(2)}) collective-permute-start(bf16[128,4096]{1,0:T(8,128)(2,1)S(1)} %get-tuple-element.14), channel_id=1, source_target_pairs={{0,128},{1,385},{2,130},{3,387},{4,132},{5,389},{6,134},{7,391},{8... | collective-permute-start | bytes 3145736 | tf_op jit(solution)/shard_map/ppermute | solution.py:37
  116.0 15.8 %collective-permute-start.18 = (bf16[128,4096]{1,0:T(8,128)(2,1)S(1)}, bf16[128,4096]{1,0:T(8,128)(2,1)S(1)}, u32[]{:S(2)}, u32[]{:S(2)}) collective-permute-start(bf16[128,4096]{1,0:T(8,128)(2,1)S(1)} %get-tuple-element.14), channel_id=1, source_target_pairs={{0,2},{1,7},{2,4},{3,1},{4,6},{5,3},{6,0},{7,5},{8,10},{9,15},{10,... | collective-permute-start | bytes 3145736 | tf_op jit(solution)/shard_map/ppermute | solution.py:37
  119.2 17.2 %collective-permute-start.19 = (bf16[128,4096]{1,0:T(8,128)(2,1)S(1)}, bf16[128,4096]{1,0:T(8,128)(2,1)S(1)}, u32[]{:S(2)}, u32[]{:S(2)}) collective-permute-start(bf16[128,4096]{1,0:T(8,128)(2,1)S(1)} %get-tuple-element.14), channel_id=1, source_target_pairs={{0,8},{1,121},{2,10},{3,123},{4,12},{5,125},{6,14},{7,127},{8,16},... | collective-permute-start | bytes 3145736 | tf_op jit(solution)/shard_map/ppermute | solution.py:37
  127.6 9.6 %copy-start.2 = (bf16[1,4096,128]{2,1,0:T(8,128)(2,1)S(1)}, bf16[1,4096,128]{2,1,0:T(8,128)(2,1)}, u32[]{:S(2)}) copy-start(bf16[1,4096,128]{2,1,0:T(8,128)(2,1)} %param.9) | copy-start | bytes 3145732
  144.2 8.5 %collective-permute-start.20 = (f32[512,256]{1,0:T(8,128)S(1)}, f32[512,256]{1,0:T(8,128)S(1)}, u32[]{:S(2)}, u32[]{:S(2)}) collective-permute-start(f32[512,256]{1,0:T(8,128)S(1)} %get-tuple-element.8), channel_id=1, source_target_pairs={{0,1},{1,0},{2,3},{3,2},{4,5},{5,4},{6,7},{7,6},{8,9},{9,8},{10,11... | collective-permute-start | bytes 1572872 | tf_op jit(solution)/shard_map/ppermute | solution.py:37
Sparse Core Ops, SparseCore 0:
  26.8 68.3 all-gather.1

commit v2 on v1

--- a/solution.py
+++ b/solution.py
@@ -73,14 +73,23 @@
     return [block] + [send(block, shift(*move)) for move in moves]
 
 
+def norm_kernel(states_ref, gain_ref, out_ref):
+    states = states_ref[...].astype(jnp.float32)
+    mean_square = jnp.mean(states * states, axis=-1, keepdims=True)
+    out_ref[...] = (states * lax.rsqrt(mean_square + 1e-06) * gain_ref[...]).astype(jnp.bfloat16)
+
+
 def attend_kernel(scale, query_ref, *refs):
     *kv_refs, own_ref, send_ref = refs
     query = query_ref[...]
+    half = HD // 2
+    keys = lambda kv: jnp.concatenate([kv[:, :half], kv[:, HD : HD + half]], axis=1)
+    values = lambda kv: jnp.concatenate([kv[:, half:HD], kv[:, HD + half :]], axis=1)
     scores = []
     for kv in kv_refs:
         scores.append(
             lax.dot_general(
-                query, kv[:, :HD], (((1,), (1,)), ((), ())), preferred_element_type=jnp.float32
+                query, keys(kv), (((1,), (1,)), ((), ())), preferred_element_type=jnp.float32
             )
             * scale
         )
@@ -90,8 +99,7 @@
     for kv, s in zip(kv_refs, scores):
         probs = jnp.exp(s - top).astype(jnp.bfloat16)
         denom += jnp.sum(probs.astype(jnp.float32), axis=-1, keepdims=True)
-        numer += jnp.dot(probs, kv[:, HD:], preferred_element_type=jnp.float32)
-    half = HD // 2
+        numer += jnp.dot(probs, values(kv), preferred_element_type=jnp.float32)
     lane = lax.broadcasted_iota(jnp.int32, (query.shape[0], half), 1)
     stats = jnp.where(lane < half // 2, top, denom)
     own_ref[:, :half] = numer[:, :half]
@@ -127,30 +135,32 @@
     seq_count = lax.axis_size(SEQ)
     half = HD // 2
 
-    states = dec_states[0].astype(jnp.float32)
-    mean_square = jnp.mean(states * states, axis=-1, keepdims=True)
-    normed = (states * lax.rsqrt(mean_square + 1e-06) * norm_gain[0]).astype(jnp.bfloat16)
+    normed = pl.pallas_call(
+        norm_kernel, out_shape=jax.ShapeDtypeStruct(dec_states.shape[1:], jnp.bfloat16)
+    )(dec_states[0], norm_gain)
+    encoder_rows, normed = lax.optimization_barrier((section_states[0], normed))
     normed_all = lax.all_gather(normed, SEQ, axis=0, tiled=True)
 
+    piece = scatter_x(encoder_rows)
+
     other_core = pairs_of(lambda x, zh, zl, y, c: (x, zh, zl, y, 1 - c))
-    mine = (w_key[0], w_value[0], w_query[0])
-    other = [send(w, other_core) for w in mine]
+    kv_mine = jnp.concatenate([w_key[0], w_value[0]], axis=1)
+    piece, kv_mine, query_mine = lax.optimization_barrier((piece, kv_mine, w_query[0]))
+    kv_other, query_other = send(kv_mine, other_core), send(query_mine, other_core)
+    piece = spread_z(piece)
+    piece, kv_other, query_other = lax.optimization_barrier((piece, kv_other, query_other))
 
-    piece = spread_z(scatter_x(section_states[0]))
     piece = jnp.concatenate(widen(piece, ((2, 2, 2), (1, 1, -1), (-1, -1, 1))), axis=0)
     quarter = jnp.concatenate(widen(piece, ((1, 0, 1), (-1, 0, -1), (0, 2, 0))), axis=0)
-    one_hop = ((1, 0, 0), (0, 1, 0), (0, 0, 1))
-    middle = quarter.shape[0] // 2
-    first = widen(quarter[:middle], one_hop)
-    second = widen(quarter[middle:], one_hop)
-    blocks = [quarter] + first[1:] + second[1:]
+    _, *arrived = widen(quarter, ((1, 0, 0), (0, 1, 0), (0, 0, 1)))
 
-    kv_cols = jnp.concatenate([mine[0], other[0], mine[1], other[1]], axis=1)
-    query_cols = jnp.concatenate([mine[2], other[2]], axis=1)
+    kv_cols = jnp.concatenate([kv_mine, kv_other], axis=1)
+    query_cols = jnp.concatenate([query_mine, query_other], axis=1)
     queries = jnp.dot(normed_all, query_cols, preferred_element_type=jnp.float32).astype(jnp.bfloat16)
-    key_values = [
-        jnp.dot(rows, kv_cols, preferred_element_type=jnp.float32).astype(jnp.bfloat16) for rows in blocks
-    ]
+    project = lambda rows: jnp.dot(rows, kv_cols, preferred_element_type=jnp.float32).astype(jnp.bfloat16)
+    near = project(quarter)
+    queries, near, *arrived = lax.optimization_barrier((queries, near, *arrived))
+    key_values = [near] + [project(rows) for rows in arrived]
 
     own, outgoing = attend(queries, key_values)
     arrived = send(outgoing, other_core)

time: 173 us -> 168 us (0.971)
  waiting for transfers between devices: 51.2 us -> 40.5 us
  starting transfers between devices: 76.3 us -> 66.1 us
  local copies, waits for them, and re-layouts: 2.18 us -> 10.9 us
  matrix products: 9.29 us -> 15 us
    ppermute x21 -> x17, waiting for transfers between devices: 51.2 us -> 40.4 us  [send(): return lax.ppermute(value, AXES, pairs)]
    ppermute x21 -> x17, starting transfers between devices: 76.3 us -> 66.1 us  [send(): return lax.ppermute(value, AXES, pairs)]
    dot_general x7 -> x4, matrix products: 5.55 us -> 11.4 us  [local(): jnp.dot(rows, kv_cols, preferred_element_type=jnp.float32)]
    unnamed x11 -> x12, local copies, waits for them, and re-layouts: 0.18 us -> 5.83 us
    concatenate x0 -> x2, local copies, waits for them, and re-layouts: none -> 2.42 us  [the longest x1 1.75 us: local(): kv_cols = jnp.concatenate([kv_mine, kv_other], axis=1)]
  transfers between devices with their start and end apart: 22 -> 18, of which waited for: 10 -> 10; matrix products, arithmetic and copies ran while one was open for 5% -> 10% of each run, Pallas kernels for 0% -> 0%
where the time goes in v2:
time: 168 us; the launch traced here: 167 us
  starting transfers between devices  66.1 us (39%)
  waiting for transfers between devices  40.5 us (24%)
  matrix products  15 us (9%)
  between operations  13.7 us (8%)
  blocking collectives  12.9 us (8%)
  local copies, waits for them, and re-layouts  10.9 us (6%)
  Pallas kernels  4.53 us (3%)
  other arithmetic  3.46 us (2%)
    ppermute x17, starting transfers between devices, send(): return lax.ppermute(value, AXES, pairs)  66.1 us
    ppermute x17, waiting for transfers between devices, send(): return lax.ppermute(value, AXES, pairs)  40.4 us
    all_to_all x1, blocking collectives, local(): lax.all_to_all(parts, SEQ, split_axis=0, concat_axis=0, tiled=True)  12.9 us
    dot_general x4, matrix products, local(): jnp.dot(rows, kv_cols, preferred_element_type=jnp.float32)  11.4 us
    unnamed x12, local copies, waits for them, and re-layouts  5.83 us
    dot_general x1, matrix products, local(): jnp.dot(normed_all, query_cols, preferred_element_type=jnp.float32)  3.58 us
  transfers between devices with their start and end apart: 18, of which 10 were waited for; matrix products, arithmetic and copies ran while one was open for 10% of the time, Pallas kernels for 0%

profile of v2, /device:TPU:1, one launch (start us, length us, event | category | flops | bytes accessed | tf_op | source)
XLA Modules:
  0.0 167.1 jit_solution(14800498627345814576)
XLA Ops:
  6.5 0.0 all-gather.2.cloned.1.call-start
  6.5 1.7 %shard_map.64 = bf16[16,4096]{1,0:T(8,128)(2,1)} custom-call(bf16[16,4096]{1,0:T(8,128)(2,1)} %bitcast.22, f32[1,4096]{1,0:T(1,128)} %gain_ref.1), custom_call_target="tpu_custom_call" | custom-call | tf_op jit(solution)/shard_map/pallas_call | solution.py:138
  8.2 0.0 all-gather.2.cloned.1.call-update
  8.3 1.1 fusion.17
  9.3 5.2 %collective-permute-start = (bf16[16,4096]{1,0:T(8,128)(2,1)S(1)}, bf16[16,4096]{1,0:T(8,128)(2,1)S(1)}, u32[]{:S(2)}, u32[]{:S(2)}) collective-permute-start(bf16[16,4096]{1,0:T(8,128)(2,1)S(1)} %get-tuple-element.40), channel_id=1, source_target_pairs={{0,384},{1,385},{2,386},{3,387},{4,388},{5,389},{6,390},{7,391},{8... | collective-permute-start | bytes 393224 | tf_op jit(solution)/shard_map/ppermute | solution.py:37
  14.6 1.3 collective-permute-start.1
  15.9 1.3 collective-permute-start.2
  17.2 1.8 %pad_maximum_fusion = bf16[4096,256]{1,0:T(8,128)(2,1)S(1)} fusion(bf16[4096,128]{1,0:T(8,128)(2,1)} %bitcast.16, bf16[4096,128]{1,0:T(8,128)(2,1)} %bitcast.17), kind=kLoop, calls=%fused_computation | loop fusion | flops 4194304 | bytes 4194304 | tf_op jit(solution)/shard_map/concatenate | solution.py:147
  19.0 0.0 collective-permute-done
  19.0 0.0 collective-permute-done.1
  19.0 0.2 collective-permute-done.2
  19.2 0.9 select_select_fusion
  20.1 5.4 %collective-permute-start.5 = (bf16[4096,256]{1,0:T(8,128)(2,1)S(1)}, bf16[4096,256]{1,0:T(8,128)(2,1)}, u32[]{:S(2)}, u32[]{:S(2)}) collective-permute-start(bf16[4096,256]{1,0:T(8,128)(2,1)S(1)} %pad_maximum_fusion), channel_id=1, source_target_pairs={{0,1},{1,0},{2,3},{3,2},{4,5},{5,4},{6,7},{7,6},{8,9},{9,8},{10,11... | collective-permute-start | bytes 6291464 | tf_op jit(solution)/shard_map/ppermute | solution.py:37
  25.5 4.5 %collective-permute-start.3 = (bf16[16,4096]{1,0:T(8,128)(2,1)S(1)}, bf16[16,4096]{1,0:T(8,128)(2,1)S(1)}, u32[]{:S(2)}, u32[]{:S(2)}) collective-permute-start(bf16[16,4096]{1,0:T(8,128)(2,1)S(1)} %select_select_fusion), channel_id=1, source_target_pairs={{0,32},{1,97},{2,34},{3,99},{4,36},{5,101},{6,38},{7,103},{8,40},{... | collective-permute-start | bytes 393224 | tf_op jit(solution)/shard_map/ppermute | solution.py:37
  30.0 1.9 %collective-permute-start.6 = (bf16[4096,128]{1,0:T(8,128)(2,1)}, bf16[4096,128]{1,0:T(8,128)(2,1)S(1)}, u32[]{:S(2)}, u32[]{:S(2)}) collective-permute-start(bf16[4096,128]{1,0:T(8,128)(2,1)} %bitcast.23), channel_id=1, source_target_pairs={{0,1},{1,0},{2,3},{3,2},{4,5},{5,4},{6,7},{7,6},{8,9},{9,8},{10,11... | collective-permute-start | bytes 3145736 | tf_op jit(solution)/shard_map/ppermute | solution.py:37
  31.9 6.2 %collective-permute-done.3 = bf16[16,4096]{1,0:T(8,128)(2,1)S(1)} collective-permute-done((bf16[16,4096]{1,0:T(8,128)(2,1)S(1)}, bf16[16,4096]{1,0:T(8,128)(2,1)S(1)}, u32[]{:S(2)}, u32[]{:S(2)}) %collective-permute-start.3) | collective-permute-done | bytes 131104 | tf_op jit(solution)/shard_map/ppermute | solution.py:37
  38.1 1.3 collective-permute-start.4
  39.5 2.8 %collective-permute-done.4 = bf16[16,4096]{1,0:T(8,128)(2,1)S(1)} collective-permute-done((bf16[16,4096]{1,0:T(8,128)(2,1)S(1)}, bf16[16,4096]{1,0:T(8,128)(2,1)S(1)}, u32[]{:S(2)}, u32[]{:S(2)}) %collective-permute-start.4) | collective-permute-done | bytes 131104 | tf_op jit(solution)/shard_map/ppermute | solution.py:37
  42.2 0.0 collective-permute-done.6
  42.2 0.0 collective-permute-done.5
  42.3 6.4 %collective-permute-start.7 = (bf16[16,4096]{1,0:T(8,128)(2,1)S(1)}, bf16[16,4096]{1,0:T(8,128)(2,1)S(1)}, u32[]{:S(2)}, u32[]{:S(2)}) collective-permute-start(bf16[16,4096]{1,0:T(8,128)(2,1)S(1)} %broadcast_select_fusion.1), channel_id=1, source_target_pairs={{0,276},{1,373},{2,278},{3,375},{4,272},{5,369},{6,274},{7,371},{8... | collective-permute-start | bytes 393224 | tf_op jit(solution)/shard_map/ppermute | solution.py:37
  48.7 0.7 constant_dynamic-update-slice_fusion.3
  49.4 4.8 %collective-permute-start.8 = (bf16[16,4096]{1,0:T(8,128)(2,1)S(1)}, bf16[16,4096]{1,0:T(8,128)(2,1)S(1)}, u32[]{:S(2)}, u32[]{:S(2)}) collective-permute-start(bf16[16,4096]{1,0:T(8,128)(2,1)S(1)} %broadcast_select_fusion.1), channel_id=1, source_target_pairs={{0,250},{1,399},{2,252},{3,393},{4,254},{5,395},{6,248},{7,397},{8... | collective-permute-start | bytes 393224 | tf_op jit(solution)/shard_map/ppermute | solution.py:37
  54.2 8.8 %collective-permute-start.9 = (bf16[16,4096]{1,0:T(8,128)(2,1)S(1)}, bf16[16,4096]{1,0:T(8,128)(2,1)S(1)}, u32[]{:S(2)}, u32[]{:S(2)}) collective-permute-start(bf16[16,4096]{1,0:T(8,128)(2,1)S(1)} %broadcast_select_fusion.1), channel_id=1, source_target_pairs={{0,398},{1,251},{2,392},{3,253},{4,394},{5,255},{6,396},{7,249},{8... | collective-permute-start | bytes 393224 | tf_op jit(solution)/shard_map/ppermute | solution.py:37
  63.0 0.0 collective-permute-done.7
  63.0 0.7 constant_dynamic-update-slice_fusion.2
  63.7 0.0 collective-permute-done.8
  63.7 0.7 constant_dynamic-update-slice_fusion.1
  64.4 0.9 collective-permute-done.9
  65.2 0.7 constant_dynamic-update-slice_fusion
  65.9 8.1 %collective-permute-start.10 = (bf16[64,4096]{1,0:T(8,128)(2,1)S(1)}, bf16[64,4096]{1,0:T(8,128)(2,1)S(1)}, u32[]{:S(2)}, u32[]{:S(2)}) collective-permute-start(bf16[64,4096]{1,0:T(8,128)(2,1)S(1)} %get-tuple-element.41), channel_id=1, source_target_pairs={{0,136},{1,505},{2,138},{3,507},{4,140},{5,509},{6,142},{7,511},{8... | collective-permute-start | bytes 1572872 | tf_op jit(solution)/shard_map/ppermute | solution.py:37
  74.0 1.9 %collective-permute-start.11 = (bf16[64,4096]{1,0:T(8,128)(2,1)S(1)}, bf16[64,4096]{1,0:T(8,128)(2,1)S(1)}, u32[]{:S(2)}, u32[]{:S(2)}) collective-permute-start(bf16[64,4096]{1,0:T(8,128)(2,1)S(1)} %get-tuple-element.41), channel_id=1, source_target_pairs={{0,504},{1,137},{2,506},{3,139},{4,508},{5,141},{6,510},{7,143},{8... | collective-permute-start | bytes 1572872 | tf_op jit(solution)/shard_map/ppermute | solution.py:37
  75.9 2.0 %collective-permute-start.12 = (bf16[64,4096]{1,0:T(8,128)(2,1)S(1)}, bf16[64,4096]{1,0:T(8,128)(2,1)S(1)}, u32[]{:S(2)}, u32[]{:S(2)}) collective-permute-start(bf16[64,4096]{1,0:T(8,128)(2,1)S(1)} %get-tuple-element.41), channel_id=1, source_target_pairs={{0,4},{1,5},{2,6},{3,7},{4,0},{5,1},{6,2},{7,3},{8,12},{9,13},{10,... | collective-permute-start | bytes 1572872 | tf_op jit(solution)/shard_map/ppermute | solution.py:37
  77.9 9.7 %collective-permute-done.10 = bf16[64,4096]{1,0:T(8,128)(2,1)S(1)} collective-permute-done((bf16[64,4096]{1,0:T(8,128)(2,1)S(1)}, bf16[64,4096]{1,0:T(8,128)(2,1)S(1)}, u32[]{:S(2)}, u32[]{:S(2)}) %collective-permute-start.10) | collective-permute-done | bytes 524320 | tf_op jit(solution)/shard_map/ppermute | solution.py:37
  87.6 0.8 constant_dynamic-update-slice_fusion.6
  88.4 0.0 collective-permute-done.11
  88.4 0.8 constant_dynamic-update-slice_fusion.5
  89.3 6.0 %collective-permute-done.12 = bf16[64,4096]{1,0:T(8,128)(2,1)S(1)} collective-permute-done((bf16[64,4096]{1,0:T(8,128)(2,1)S(1)}, bf16[64,4096]{1,0:T(8,128)(2,1)S(1)}, u32[]{:S(2)}, u32[]{:S(2)}) %collective-permute-start.12) | collective-permute-done | bytes 524320 | tf_op jit(solution)/shard_map/ppermute | solution.py:37
  95.3 0.8 constant_dynamic-update-slice_fusion.4
  96.1 4.1 %collective-permute-start.13 = (bf16[256,4096]{1,0:T(8,128)(2,1)}, bf16[256,4096]{1,0:T(8,128)(2,1)}, u32[]{:S(2)}, u32[]{:S(2)}) collective-permute-start(bf16[256,4096]{1,0:T(8,128)(2,1)} %constant_dynamic-update-slice_fusion.4), channel_id=1, source_target_pairs={{0,128},{1,385},{2,130},{3,387},{4,132},{5,389},{6,134},{7,391},{8... | collective-permute-start | bytes 6291464 | tf_op jit(solution)/shard_map/ppermute | solution.py:37
  100.2 2.6 %collective-permute-start.14 = (bf16[256,4096]{1,0:T(8,128)(2,1)}, bf16[256,4096]{1,0:T(8,128)(2,1)}, u32[]{:S(2)}, u32[]{:S(2)}) collective-permute-start(bf16[256,4096]{1,0:T(8,128)(2,1)} %constant_dynamic-update-slice_fusion.4), channel_id=1, source_target_pairs={{0,2},{1,7},{2,4},{3,1},{4,6},{5,3},{6,0},{7,5},{8,10},{9,15},{10,... | collective-permute-start | bytes 6291464 | tf_op jit(solution)/shard_map/ppermute | solution.py:37
  102.9 3.6 %collective-permute-start.15 = (bf16[256,4096]{1,0:T(8,128)(2,1)}, bf16[256,4096]{1,0:T(8,128)(2,1)}, u32[]{:S(2)}, u32[]{:S(2)}) collective-permute-start(bf16[256,4096]{1,0:T(8,128)(2,1)} %constant_dynamic-update-slice_fusion.4), channel_id=1, source_target_pairs={{0,8},{1,121},{2,10},{3,123},{4,12},{5,125},{6,14},{7,127},{8,16},... | collective-permute-start | bytes 6291464 | tf_op jit(solution)/shard_map/ppermute | solution.py:37
  106.5 0.2 constant_dynamic-update-slice_fusion.12
  106.7 1.8 %constant_dynamic-update-slice_fusion.11 = bf16[4096,512]{1,0:T(8,128)(2,1)S(1)} fusion(bf16[4096,512]{1,0:T(8,128)(2,1)S(1)} %constant_dynamic-update-slice_fusion.12, bf16[4096,256]{1,0:T(8,128)(2,1)} %collective-permute-done.5), kind=kLoop, calls=%fused_computation.37 | loop fusion | bytes 4194304 | tf_op jit(solution)/shard_map/concatenate | solution.py:157
  108.4 0.0 copy-start
  108.5 2.0 %copy-done = bf16[4096,512]{1,0:T(8,128)(2,1)} copy-done((bf16[4096,512]{1,0:T(8,128)(2,1)}, bf16[4096,512]{1,0:T(8,128)(2,1)S(1)}, u32[]{:S(2)}) %copy-start) | copy-done | bytes 4194328
  110.4 2.9 %convolution_convert_fusion.3.refs_0_ = bf16[256,512]{1,0:T(8,128)(2,1)S(1)} fusion(bf16[256,4096]{1,0:T(8,128)(2,1)} %constant_dynamic-update-slice_fusion.4, bf16[4096,512]{1,0:T(8,128)(2,1)S(1)} %constant_dynamic-update-slice_fusion.11), kind=kOutput, calls=%fused_computation.9 | convolution fusion | flops 1073872896 | bytes 6553600 | tf_op jit(solution)/shard_map/dot_general | solution.py:160
  113.4 0.0 all-gather.2.cloned.1.call-done
  113.4 0.0 copy-done.2
  113.4 0.0 copy-start.1
  113.4 3.6 %fusion.4.query_ref = bf16[512,256]{1,0:T(8,128)(2,1)S(1)} fusion(bf16[512,4096]{1,0:T(8,128)(2,1)} %all-gather.2.cloned.1.call-done, bf16[4096,128]{1,0:T(8,128)(2,1)S(1)} %collective-permute-done.6, bf16[4096,128]{1,0:T(8,128)(2,1)S(1)} %bitcast.24), kind=kOutput, calls=%fused_computation.5 | convolution fusion | flops 1078067200 | bytes 6553600 | tf_op jit(solution)/shard_map/dot_general | solution.py:159
  117.0 6.5 %collective-permute-done.13 = bf16[256,4096]{1,0:T(8,128)(2,1)} collective-permute-done((bf16[256,4096]{1,0:T(8,128)(2,1)}, bf16[256,4096]{1,0:T(8,128)(2,1)}, u32[]{:S(2)}, u32[]{:S(2)}) %collective-permute-start.13) | collective-permute-done | bytes 2097184 | tf_op jit(solution)/shard_map/ppermute | solution.py:37
  123.5 4.1 %collective-permute-done.14 = bf16[256,4096]{1,0:T(8,128)(2,1)} collective-permute-done((bf16[256,4096]{1,0:T(8,128)(2,1)}, bf16[256,4096]{1,0:T(8,128)(2,1)}, u32[]{:S(2)}, u32[]{:S(2)}) %collective-permute-start.14) | collective-permute-done | bytes 2097184 | tf_op jit(solution)/shard_map/ppermute | solution.py:37
  127.6 2.6 %collective-permute-done.15 = bf16[256,4096]{1,0:T(8,128)(2,1)} collective-permute-done((bf16[256,4096]{1,0:T(8,128)(2,1)}, bf16[256,4096]{1,0:T(8,128)(2,1)}, u32[]{:S(2)}, u32[]{:S(2)}) %collective-permute-start.15) | collective-permute-done | bytes 2097184 | tf_op jit(solution)/shard_map/ppermute | solution.py:37
  130.3 2.8 %convolution_convert_fusion.2.refs_1_ = bf16[256,512]{1,0:T(8,128)(2,1)S(1)} fusion(bf16[256,4096]{1,0:T(8,128)(2,1)} %collective-permute-done.13, bf16[4096,512]{1,0:T(8,128)(2,1)S(1)} %copy-done.1), kind=kOutput, calls=%fused_computation.8 | convolution fusion | flops 1073872896 | bytes 6553600 | tf_op jit(solution)/shard_map/dot_general | solution.py:160
  133.1 2.8 %convolution_convert_fusion.1.refs_2_ = bf16[256,512]{1,0:T(8,128)(2,1)S(1)} fusion(bf16[256,4096]{1,0:T(8,128)(2,1)} %collective-permute-done.14, bf16[4096,512]{1,0:T(8,128)(2,1)S(1)} %copy-done.1), kind=kOutput, calls=%fused_computation.7 | convolution fusion | flops 1073872896 | bytes 6553600 | tf_op jit(solution)/shard_map/dot_general | solution.py:160
  135.9 2.8 %convolution_convert_fusion.refs_3_ = bf16[256,512]{1,0:T(8,128)(2,1)S(1)} fusion(bf16[256,4096]{1,0:T(8,128)(2,1)} %collective-permute-done.15, bf16[4096,512]{1,0:T(8,128)(2,1)S(1)} %copy-done.1), kind=kOutput, calls=%fused_computation.6 | convolution fusion | flops 1073872896 | bytes 6553600 | tf_op jit(solution)/shard_map/dot_general | solution.py:160
  138.8 2.8 %shard_map.65 = (f32[512,256]{1,0:T(8,128)S(1)}, f32[512,256]{1,0:T(8,128)S(1)}) custom-call(bf16[512,256]{1,0:T(8,128)(2,1)S(1)} %fusion.4.query_ref, bf16[256,512]{1,0:T(8,128)(2,1)S(1)} %convolution_convert_fusion.3.refs_0_, bf16[256,512]{1,0:T(8,128)(2,1)S(1)} %convolution_convert_fusion.2.refs_1_, ...), custom_call_target="tpu_custom_call" | custom-call | flops 536870912 | bytes 2359296 | tf_op jit(solution)/shard_map/pallas_call | solution.py:117
  141.6 2.7 %collective-permute-start.16 = (f32[512,256]{1,0:T(8,128)S(1)}, f32[512,256]{1,0:T(8,128)S(1)}, u32[]{:S(2)}, u32[]{:S(2)}) collective-permute-start(f32[512,256]{1,0:T(8,128)S(1)} %get-tuple-element.34), channel_id=1, source_target_pairs={{0,1},{1,0},{2,3},{3,2},{4,5},{5,4},{6,7},{7,6},{8,9},{9,8},{10,11... | collective-permute-start | bytes 1572872 | tf_op jit(solution)/shard_map/ppermute | solution.py:37
  144.3 1.5 collective-permute-done.16
  145.8 0.5 fusion.15
  146.2 0.3 fusion.13
  146.5 12.9 %all_to_all.5 = bf16[32,16,128]{2,1,0:T(8,128)(2,1)S(1)} all-to-all(bf16[32,16,128]{2,1,0:T(8,128)(2,1)S(1)} %bitcast.18), channel_id=1, replica_groups=mesh['x'=4,'zh'=4,'zl'=4,'y'=4,'core'=2] {'zl','y','core'}, dimensions={0} | all-to-all | bytes 262144 | tf_op jit(solution)/shard_map/all_to_all | solution.py:175
  159.5 0.7 reshape.7
  (5 shorter events, 0.1 us)
Async XLA Ops:
  6.5 106.9 %all-gather.2.cloned.1.call-start = ((), (), s32[]{:S(2)}) async-start(), calls=%async_computation.1 | async-start | bytes 4325376 | tf_op jit(solution)/shard_map/all_gather | solution.py:142
  9.3 9.6 %collective-permute-start = (bf16[16,4096]{1,0:T(8,128)(2,1)S(1)}, bf16[16,4096]{1,0:T(8,128)(2,1)S(1)}, u32[]{:S(2)}, u32[]{:S(2)}) collective-permute-start(bf16[16,4096]{1,0:T(8,128)(2,1)S(1)} %get-tuple-element.40), channel_id=1, source_target_pairs={{0,384},{1,385},{2,386},{3,387},{4,388},{5,389},{6,390},{7,391},{8... | collective-permute-start | bytes 393224 | tf_op jit(solution)/shard_map/ppermute | solution.py:37
  14.6 4.4 %collective-permute-start.1 = (bf16[16,4096]{1,0:T(8,128)(2,1)S(1)}, bf16[16,4096]{1,0:T(8,128)(2,1)S(1)}, u32[]{:S(2)}, u32[]{:S(2)}) collective-permute-start(bf16[16,4096]{1,0:T(8,128)(2,1)S(1)} %get-tuple-element.39), channel_id=1, source_target_pairs={{0,128},{1,129},{2,130},{3,131},{4,132},{5,133},{6,134},{7,135},{8... | collective-permute-start | bytes 393224 | tf_op jit(solution)/shard_map/ppermute | solution.py:37
  15.9 3.3 %collective-permute-start.2 = (bf16[16,4096]{1,0:T(8,128)(2,1)S(1)}, bf16[16,4096]{1,0:T(8,128)(2,1)S(1)}, u32[]{:S(2)}, u32[]{:S(2)}) collective-permute-start(bf16[16,4096]{1,0:T(8,128)(2,1)S(1)} %get-tuple-element.38), channel_id=1, source_target_pairs={{0,256},{1,257},{2,258},{3,259},{4,260},{5,261},{6,262},{7,263},{8... | collective-permute-start | bytes 393224 | tf_op jit(solution)/shard_map/ppermute | solution.py:37
  20.1 22.2 %collective-permute-start.5 = (bf16[4096,256]{1,0:T(8,128)(2,1)S(1)}, bf16[4096,256]{1,0:T(8,128)(2,1)}, u32[]{:S(2)}, u32[]{:S(2)}) collective-permute-start(bf16[4096,256]{1,0:T(8,128)(2,1)S(1)} %pad_maximum_fusion), channel_id=1, source_target_pairs={{0,1},{1,0},{2,3},{3,2},{4,5},{5,4},{6,7},{7,6},{8,9},{9,8},{10,11... | collective-permute-start | bytes 6291464 | tf_op jit(solution)/shard_map/ppermute | solution.py:37
  25.5 12.6 %collective-permute-start.3 = (bf16[16,4096]{1,0:T(8,128)(2,1)S(1)}, bf16[16,4096]{1,0:T(8,128)(2,1)S(1)}, u32[]{:S(2)}, u32[]{:S(2)}) collective-permute-start(bf16[16,4096]{1,0:T(8,128)(2,1)S(1)} %select_select_fusion), channel_id=1, source_target_pairs={{0,32},{1,97},{2,34},{3,99},{4,36},{5,101},{6,38},{7,103},{8,40},{... | collective-permute-start | bytes 393224 | tf_op jit(solution)/shard_map/ppermute | solution.py:37
  30.0 12.2 %collective-permute-start.6 = (bf16[4096,128]{1,0:T(8,128)(2,1)}, bf16[4096,128]{1,0:T(8,128)(2,1)S(1)}, u32[]{:S(2)}, u32[]{:S(2)}) collective-permute-start(bf16[4096,128]{1,0:T(8,128)(2,1)} %bitcast.23), channel_id=1, source_target_pairs={{0,1},{1,0},{2,3},{3,2},{4,5},{5,4},{6,7},{7,6},{8,9},{9,8},{10,11... | collective-permute-start | bytes 3145736 | tf_op jit(solution)/shard_map/ppermute | solution.py:37
  38.1 4.1 %collective-permute-start.4 = (bf16[16,4096]{1,0:T(8,128)(2,1)S(1)}, bf16[16,4096]{1,0:T(8,128)(2,1)S(1)}, u32[]{:S(2)}, u32[]{:S(2)}) collective-permute-start(bf16[16,4096]{1,0:T(8,128)(2,1)S(1)} %broadcast_select_fusion), channel_id=1, source_target_pairs={{0,96},{1,33},{2,98},{3,35},{4,100},{5,37},{6,102},{7,39},{8,104},... | collective-permute-start | bytes 393224 | tf_op jit(solution)/shard_map/ppermute | solution.py:37
  42.3 20.8 %collective-permute-start.7 = (bf16[16,4096]{1,0:T(8,128)(2,1)S(1)}, bf16[16,4096]{1,0:T(8,128)(2,1)S(1)}, u32[]{:S(2)}, u32[]{:S(2)}) collective-permute-start(bf16[16,4096]{1,0:T(8,128)(2,1)S(1)} %broadcast_select_fusion.1), channel_id=1, source_target_pairs={{0,276},{1,373},{2,278},{3,375},{4,272},{5,369},{6,274},{7,371},{8... | collective-permute-start | bytes 393224 | tf_op jit(solution)/shard_map/ppermute | solution.py:37
  49.4 14.3 %collective-permute-start.8 = (bf16[16,4096]{1,0:T(8,128)(2,1)S(1)}, bf16[16,4096]{1,0:T(8,128)(2,1)S(1)}, u32[]{:S(2)}, u32[]{:S(2)}) collective-permute-start(bf16[16,4096]{1,0:T(8,128)(2,1)S(1)} %broadcast_select_fusion.1), channel_id=1, source_target_pairs={{0,250},{1,399},{2,252},{3,393},{4,254},{5,395},{6,248},{7,397},{8... | collective-permute-start | bytes 393224 | tf_op jit(solution)/shard_map/ppermute | solution.py:37
  54.2 11.0 %collective-permute-start.9 = (bf16[16,4096]{1,0:T(8,128)(2,1)S(1)}, bf16[16,4096]{1,0:T(8,128)(2,1)S(1)}, u32[]{:S(2)}, u32[]{:S(2)}) collective-permute-start(bf16[16,4096]{1,0:T(8,128)(2,1)S(1)} %broadcast_select_fusion.1), channel_id=1, source_target_pairs={{0,398},{1,251},{2,392},{3,253},{4,394},{5,255},{6,396},{7,249},{8... | collective-permute-start | bytes 393224 | tf_op jit(solution)/shard_map/ppermute | solution.py:37
  65.9 21.7 %collective-permute-start.10 = (bf16[64,4096]{1,0:T(8,128)(2,1)S(1)}, bf16[64,4096]{1,0:T(8,128)(2,1)S(1)}, u32[]{:S(2)}, u32[]{:S(2)}) collective-permute-start(bf16[64,4096]{1,0:T(8,128)(2,1)S(1)} %get-tuple-element.41), channel_id=1, source_target_pairs={{0,136},{1,505},{2,138},{3,507},{4,140},{5,509},{6,142},{7,511},{8... | collective-permute-start | bytes 1572872 | tf_op jit(solution)/shard_map/ppermute | solution.py:37
  74.0 14.5 %collective-permute-start.11 = (bf16[64,4096]{1,0:T(8,128)(2,1)S(1)}, bf16[64,4096]{1,0:T(8,128)(2,1)S(1)}, u32[]{:S(2)}, u32[]{:S(2)}) collective-permute-start(bf16[64,4096]{1,0:T(8,128)(2,1)S(1)} %get-tuple-element.41), channel_id=1, source_target_pairs={{0,504},{1,137},{2,506},{3,139},{4,508},{5,141},{6,510},{7,143},{8... | collective-permute-start | bytes 1572872 | tf_op jit(solution)/shard_map/ppermute | solution.py:37
  75.9 19.3 %collective-permute-start.12 = (bf16[64,4096]{1,0:T(8,128)(2,1)S(1)}, bf16[64,4096]{1,0:T(8,128)(2,1)S(1)}, u32[]{:S(2)}, u32[]{:S(2)}) collective-permute-start(bf16[64,4096]{1,0:T(8,128)(2,1)S(1)} %get-tuple-element.41), channel_id=1, source_target_pairs={{0,4},{1,5},{2,6},{3,7},{4,0},{5,1},{6,2},{7,3},{8,12},{9,13},{10,... | collective-permute-start | bytes 1572872 | tf_op jit(solution)/shard_map/ppermute | solution.py:37
  96.1 27.4 %collective-permute-start.13 = (bf16[256,4096]{1,0:T(8,128)(2,1)}, bf16[256,4096]{1,0:T(8,128)(2,1)}, u32[]{:S(2)}, u32[]{:S(2)}) collective-permute-start(bf16[256,4096]{1,0:T(8,128)(2,1)} %constant_dynamic-update-slice_fusion.4), channel_id=1, source_target_pairs={{0,128},{1,385},{2,130},{3,387},{4,132},{5,389},{6,134},{7,391},{8... | collective-permute-start | bytes 6291464 | tf_op jit(solution)/shard_map/ppermute | solution.py:37
  100.2 27.4 %collective-permute-start.14 = (bf16[256,4096]{1,0:T(8,128)(2,1)}, bf16[256,4096]{1,0:T(8,128)(2,1)}, u32[]{:S(2)}, u32[]{:S(2)}) collective-permute-start(bf16[256,4096]{1,0:T(8,128)(2,1)} %constant_dynamic-update-slice_fusion.4), channel_id=1, source_target_pairs={{0,2},{1,7},{2,4},{3,1},{4,6},{5,3},{6,0},{7,5},{8,10},{9,15},{10,... | collective-permute-start | bytes 6291464 | tf_op jit(solution)/shard_map/ppermute | solution.py:37
  102.9 27.4 %collective-permute-start.15 = (bf16[256,4096]{1,0:T(8,128)(2,1)}, bf16[256,4096]{1,0:T(8,128)(2,1)}, u32[]{:S(2)}, u32[]{:S(2)}) collective-permute-start(bf16[256,4096]{1,0:T(8,128)(2,1)} %constant_dynamic-update-slice_fusion.4), channel_id=1, source_target_pairs={{0,8},{1,121},{2,10},{3,123},{4,12},{5,125},{6,14},{7,127},{8,16},... | collective-permute-start | bytes 6291464 | tf_op jit(solution)/shard_map/ppermute | solution.py:37
  108.4 2.0 %copy-start = (bf16[4096,512]{1,0:T(8,128)(2,1)}, bf16[4096,512]{1,0:T(8,128)(2,1)S(1)}, u32[]{:S(2)}) copy-start(bf16[4096,512]{1,0:T(8,128)(2,1)S(1)} %constant_dynamic-update-slice_fusion.11) | copy-start | bytes 12582916
  110.4 3.0 %copy-start.2 = (bf16[1,4096,128]{2,1,0:T(8,128)(2,1)S(1)}, bf16[1,4096,128]{2,1,0:T(8,128)(2,1)}, u32[]{:S(2)}) copy-start(bf16[1,4096,128]{2,1,0:T(8,128)(2,1)} %param.9) | copy-start | bytes 3145732
  113.4 16.8 %copy-start.1 = (bf16[4096,512]{1,0:T(8,128)(2,1)S(1)}, bf16[4096,512]{1,0:T(8,128)(2,1)}, u32[]{:S(2)}) copy-start(bf16[4096,512]{1,0:T(8,128)(2,1)} %copy-done) | copy-start | bytes 12582916
  141.6 4.2 %collective-permute-start.16 = (f32[512,256]{1,0:T(8,128)S(1)}, f32[512,256]{1,0:T(8,128)S(1)}, u32[]{:S(2)}, u32[]{:S(2)}) collective-permute-start(f32[512,256]{1,0:T(8,128)S(1)} %get-tuple-element.34), channel_id=1, source_target_pairs={{0,1},{1,0},{2,3},{3,2},{4,5},{5,4},{6,7},{7,6},{8,9},{9,8},{10,11... | collective-permute-start | bytes 1572872 | tf_op jit(solution)/shard_map/ppermute | solution.py:37
Sparse Core Ops, SparseCore 0:
  9.5 83.4 all-gather.1

commit v3 on v2

--- a/solution.py
+++ b/solution.py
@@ -120,7 +120,7 @@
         grid=(count // block,),
         in_specs=[row_spec] + [pl.BlockSpec(kv.shape, lambda i: (0, 0)) for kv in key_values],
         out_specs=(row_spec, row_spec),
-        compiler_params=pltpu.CompilerParams(vmem_limit_bytes=40 * 2**20),
+        compiler_params=pltpu.CompilerParams(vmem_limit_bytes=16 * 2**20),
         cost_estimate=pl.CostEstimate(
             flops=4 * count * keys * HD,
             bytes_accessed=keys * HD * 4 + count * HD * 10,
@@ -136,7 +136,9 @@
     half = HD // 2
 
     normed = pl.pallas_call(
-        norm_kernel, out_shape=jax.ShapeDtypeStruct(dec_states.shape[1:], jnp.bfloat16)
+        norm_kernel,
+        out_shape=jax.ShapeDtypeStruct(dec_states.shape[1:], jnp.bfloat16),
+        compiler_params=pltpu.CompilerParams(vmem_limit_bytes=4 * 2**20),
     )(dec_states[0], norm_gain)
     encoder_rows, normed = lax.optimization_barrier((section_states[0], normed))
     normed_all = lax.all_gather(normed, SEQ, axis=0, tiled=True)
@@ -145,22 +147,24 @@
 
     other_core = pairs_of(lambda x, zh, zl, y, c: (x, zh, zl, y, 1 - c))
     kv_mine = jnp.concatenate([w_key[0], w_value[0]], axis=1)
-    piece, kv_mine, query_mine = lax.optimization_barrier((piece, kv_mine, w_query[0]))
+    query_mine = w_query[0]
     kv_other, query_other = send(kv_mine, other_core), send(query_mine, other_core)
     piece = spread_z(piece)
-    piece, kv_other, query_other = lax.optimization_barrier((piece, kv_other, query_other))
 
     piece = jnp.concatenate(widen(piece, ((2, 2, 2), (1, 1, -1), (-1, -1, 1))), axis=0)
-    quarter = jnp.concatenate(widen(piece, ((1, 0, 1), (-1, 0, -1), (0, 2, 0))), axis=0)
-    _, *arrived = widen(quarter, ((1, 0, 0), (0, 1, 0), (0, 0, 1)))
+    _, a, b, c = widen(piece, ((1, 0, 1), (-1, 0, -1), (0, 2, 0)))
+    one_hop = ((1, 0, 0), (0, 1, 0), (0, 0, 1))
+    near_first, *first = widen(jnp.concatenate([piece, a], axis=0), one_hop)
+    near_second, *second = widen(jnp.concatenate([b, c], axis=0), one_hop)
 
     kv_cols = jnp.concatenate([kv_mine, kv_other], axis=1)
     query_cols = jnp.concatenate([query_mine, query_other], axis=1)
     queries = jnp.dot(normed_all, query_cols, preferred_element_type=jnp.float32).astype(jnp.bfloat16)
     project = lambda rows: jnp.dot(rows, kv_cols, preferred_element_type=jnp.float32).astype(jnp.bfloat16)
-    near = project(quarter)
-    queries, near, *arrived = lax.optimization_barrier((queries, near, *arrived))
-    key_values = [near] + [project(rows) for rows in arrived]
+    blocks = [near_first, near_second] + first
+    for rows in second:
+        blocks.append(lax.optimization_barrier((rows, queries))[0])
+    key_values = [project(rows) for rows in blocks]
 
     own, outgoing = attend(queries, key_values)
     arrived = send(outgoing, other_core)

time: 168 us -> 169 us (level)
  starting transfers between devices: 66.1 us -> 84.1 us
  waiting for transfers between devices: 40.5 us -> 28 us
  local copies, waits for them, and re-layouts: 10.9 us -> 5.18 us
    ppermute x17 -> x20, starting transfers between devices: 66.1 us -> 84.1 us  [send(): return lax.ppermute(value, AXES, pairs)]
    ppermute x17 -> x20, waiting for transfers between devices: 40.4 us -> 27.9 us  [send(): return lax.ppermute(value, AXES, pairs)]
    unnamed x12 -> x16, local copies, waits for them, and re-layouts: 5.83 us -> 2.51 us
    concatenate x3 -> x2, local copies, waits for them, and re-layouts: 3.25 us -> 0.86 us  [the longest x1 0.83 us: local(): near_second, *second = widen(jnp.concatenate([b, c], axis=0), one_hop)]
    dot_general x4 -> x8, matrix products: 11.4 us -> 11.4 us  [local(): jnp.dot(rows, kv_cols, preferred_element_type=jnp.float32)]
  transfers between devices with their start and end apart: 18 -> 21, of which waited for: 10 -> 8; matrix products, arithmetic and copies ran while one was open for 10% -> 8% of each run, Pallas kernels for 0% -> 0%
where the time goes in v3:
time: 169 us; the launch traced here: 168 us
  starting transfers between devices  84.1 us (50%)
  waiting for transfers between devices  28 us (17%)
  matrix products  15.5 us (9%)
  between operations  13.9 us (8%)
  blocking collectives  13.4 us (8%)
  local copies, waits for them, and re-layouts  5.18 us (3%)
  Pallas kernels  4.27 us (3%)
  other arithmetic  3.68 us (2%)
    ppermute x20, starting transfers between devices, send(): return lax.ppermute(value, AXES, pairs)  84.1 us
    ppermute x20, waiting for transfers between devices, send(): return lax.ppermute(value, AXES, pairs)  27.9 us
    all_to_all x1, blocking collectives, local(): lax.all_to_all(parts, SEQ, split_axis=0, concat_axis=0, tiled=True)  13.4 us
    dot_general x8, matrix products, local(): jnp.dot(rows, kv_cols, preferred_element_type=jnp.float32)  11.4 us
    dot_general x1, matrix products, local(): jnp.dot(normed_all, query_cols, preferred_element_type=jnp.float32)  4.18 us
    pallas_call x1, Pallas kernels, attend(): pl.pallas_call(functools.partial(attend_kernel, HD ** (-0.5)), out_shape=...  3.47 us
  transfers between devices with their start and end apart: 21, of which 8 were waited for; matrix products, arithmetic and copies ran while one was open for 8% of the time, Pallas kernels for 0%

profile of v3, /device:TPU:1, one launch (start us, length us, event | category | flops | bytes accessed | tf_op | source)
XLA Modules:
  0.0 168.0 jit_solution(6245076022767398876)
XLA Ops:
  6.5 0.9 copy-done
  7.4 0.7 copy-done.1
  8.2 0.8 shard_map.64
  9.0 1.1 fusion.17
  10.0 5.2 %collective-permute-start.1 = (bf16[16,4096]{1,0:T(8,128)(2,1)S(1)}, bf16[16,4096]{1,0:T(8,128)(2,1)S(1)}, u32[]{:S(2)}, u32[]{:S(2)}) collective-permute-start(bf16[16,4096]{1,0:T(8,128)(2,1)S(1)} %get-tuple-element.26), channel_id=1, source_target_pairs={{0,384},{1,385},{2,386},{3,387},{4,388},{5,389},{6,390},{7,391},{8... | collective-permute-start | bytes 393224 | tf_op jit(solution)/shard_map/ppermute | solution.py:37
  15.2 1.3 collective-permute-start.2
  16.6 1.3 collective-permute-start.3
  17.9 0.0 all-gather.2.cloned.1.call-update
  17.9 0.0 collective-permute-done.1
  17.9 0.6 collective-permute-done.2
  18.5 1.4 collective-permute-done.3
  19.8 0.9 select_select_fusion
  20.8 5.6 %collective-permute-start.4 = (bf16[16,4096]{1,0:T(8,128)(2,1)S(1)}, bf16[16,4096]{1,0:T(8,128)(2,1)S(1)}, u32[]{:S(2)}, u32[]{:S(2)}) collective-permute-start(bf16[16,4096]{1,0:T(8,128)(2,1)S(1)} %select_select_fusion), channel_id=1, source_target_pairs={{0,32},{1,97},{2,34},{3,99},{4,36},{5,101},{6,38},{7,103},{8,40},{... | collective-permute-start | bytes 393224 | tf_op jit(solution)/shard_map/ppermute | solution.py:37
  26.4 8.1 %collective-permute-done.4 = bf16[16,4096]{1,0:T(8,128)(2,1)S(1)} collective-permute-done((bf16[16,4096]{1,0:T(8,128)(2,1)S(1)}, bf16[16,4096]{1,0:T(8,128)(2,1)S(1)}, u32[]{:S(2)}, u32[]{:S(2)}) %collective-permute-start.4) | collective-permute-done | bytes 131104 | tf_op jit(solution)/shard_map/ppermute | solution.py:37
  34.5 1.3 collective-permute-start.5
  35.8 1.9 %collective-permute-start = (bf16[4096,128]{1,0:T(8,128)(2,1)}, bf16[4096,128]{1,0:T(8,128)(2,1)}, u32[]{:S(2)}, u32[]{:S(2)}) collective-permute-start(bf16[4096,128]{1,0:T(8,128)(2,1)} %bitcast.39), channel_id=1, source_target_pairs={{0,1},{1,0},{2,3},{3,2},{4,5},{5,4},{6,7},{7,6},{8,9},{9,8},{10,11... | collective-permute-start | bytes 3145736 | tf_op jit(solution)/shard_map/ppermute | solution.py:37
  37.8 0.4 collective-permute-done.5
  38.2 10.2 %collective-permute-start.6 = (bf16[16,4096]{1,0:T(8,128)(2,1)S(1)}, bf16[16,4096]{1,0:T(8,128)(2,1)S(1)}, u32[]{:S(2)}, u32[]{:S(2)}) collective-permute-start(bf16[16,4096]{1,0:T(8,128)(2,1)S(1)} %get-tuple-element.23), channel_id=1, source_target_pairs={{0,276},{1,373},{2,278},{3,375},{4,272},{5,369},{6,274},{7,371},{8... | collective-permute-start | bytes 393224 | tf_op jit(solution)/shard_map/ppermute | solution.py:37
  48.4 3.3 %collective-permute-start.7 = (bf16[16,4096]{1,0:T(8,128)(2,1)S(1)}, bf16[16,4096]{1,0:T(8,128)(2,1)S(1)}, u32[]{:S(2)}, u32[]{:S(2)}) collective-permute-start(bf16[16,4096]{1,0:T(8,128)(2,1)S(1)} %get-tuple-element.23), channel_id=1, source_target_pairs={{0,250},{1,399},{2,252},{3,393},{4,254},{5,395},{6,248},{7,397},{8... | collective-permute-start | bytes 393224 | tf_op jit(solution)/shard_map/ppermute | solution.py:37
  51.7 6.3 %collective-permute-start.8 = (bf16[16,4096]{1,0:T(8,128)(2,1)S(1)}, bf16[16,4096]{1,0:T(8,128)(2,1)S(1)}, u32[]{:S(2)}, u32[]{:S(2)}) collective-permute-start(bf16[16,4096]{1,0:T(8,128)(2,1)S(1)} %get-tuple-element.23), channel_id=1, source_target_pairs={{0,398},{1,251},{2,392},{3,253},{4,394},{5,255},{6,396},{7,249},{8... | collective-permute-start | bytes 393224 | tf_op jit(solution)/shard_map/ppermute | solution.py:37
  58.0 0.0 copy-start.2
  58.0 0.0 copy-start.3
  58.0 1.9 %pad_maximum_fusion.1 = bf16[4096,256]{1,0:T(8,128)(2,1)S(1)} fusion(bf16[4096,128]{1,0:T(8,128)(2,1)} %bitcast.17, bf16[4096,128]{1,0:T(8,128)(2,1)} %bitcast.26), kind=kLoop, calls=%fused_computation.5 | loop fusion | flops 4194304 | bytes 4194304 | tf_op jit(solution)/shard_map/concatenate | solution.py:149
  60.0 1.9 %collective-permute-start.10 = (bf16[4096,256]{1,0:T(8,128)(2,1)S(1)}, bf16[4096,256]{1,0:T(8,128)(2,1)S(1)}, u32[]{:S(2)}, u32[]{:S(2)}) collective-permute-start(bf16[4096,256]{1,0:T(8,128)(2,1)S(1)} %pad_maximum_fusion.1), channel_id=1, source_target_pairs={{0,1},{1,0},{2,3},{3,2},{4,5},{5,4},{6,7},{7,6},{8,9},{9,8},{10,11... | collective-permute-start | bytes 6291464 | tf_op jit(solution)/shard_map/ppermute | solution.py:37
  61.9 0.0 collective-permute-done.6
  61.9 0.0 collective-permute-done.7
  62.0 3.8 %collective-permute-start.9 = (bf16[64,4096]{1,0:T(8,128)(2,1)S(1)}, bf16[64,4096]{1,0:T(8,128)(2,1)S(1)}, u32[]{:S(2)}, u32[]{:S(2)}) collective-permute-start(bf16[64,4096]{1,0:T(8,128)(2,1)S(1)} %pad_maximum_fusion.2), channel_id=1, source_target_pairs={{0,136},{1,505},{2,138},{3,507},{4,140},{5,509},{6,142},{7,511},{8... | collective-permute-start | bytes 1572872 | tf_op jit(solution)/shard_map/ppermute | solution.py:37
  65.8 2.4 %collective-permute-start.11 = (bf16[64,4096]{1,0:T(8,128)(2,1)S(1)}, bf16[64,4096]{1,0:T(8,128)(2,1)S(1)}, u32[]{:S(2)}, u32[]{:S(2)}) collective-permute-start(bf16[64,4096]{1,0:T(8,128)(2,1)S(1)} %pad_maximum_fusion.2), channel_id=1, source_target_pairs={{0,504},{1,137},{2,506},{3,139},{4,508},{5,141},{6,510},{7,143},{8... | collective-permute-start | bytes 1572872 | tf_op jit(solution)/shard_map/ppermute | solution.py:37
  68.2 4.4 %collective-permute-start.12 = (bf16[64,4096]{1,0:T(8,128)(2,1)S(1)}, bf16[64,4096]{1,0:T(8,128)(2,1)S(1)}, u32[]{:S(2)}, u32[]{:S(2)}) collective-permute-start(bf16[64,4096]{1,0:T(8,128)(2,1)S(1)} %pad_maximum_fusion.2), channel_id=1, source_target_pairs={{0,4},{1,5},{2,6},{3,7},{4,0},{5,1},{6,2},{7,3},{8,12},{9,13},{10,... | collective-permute-start | bytes 1572872 | tf_op jit(solution)/shard_map/ppermute | solution.py:37
  72.6 9.8 %collective-permute-done.9 = bf16[64,4096]{1,0:T(8,128)(2,1)S(1)} collective-permute-done((bf16[64,4096]{1,0:T(8,128)(2,1)S(1)}, bf16[64,4096]{1,0:T(8,128)(2,1)S(1)}, u32[]{:S(2)}, u32[]{:S(2)}) %collective-permute-start.9) | collective-permute-done | bytes 524320 | tf_op jit(solution)/shard_map/ppermute | solution.py:37
  82.5 3.9 %collective-permute-start.13 = (bf16[128,4096]{1,0:T(8,128)(2,1)S(1)}, bf16[128,4096]{1,0:T(8,128)(2,1)S(1)}, u32[]{:S(2)}, u32[]{:S(2)}) collective-permute-start(bf16[128,4096]{1,0:T(8,128)(2,1)S(1)} %constant_dynamic-update-slice_fusion), channel_id=1, source_target_pairs={{0,128},{1,385},{2,130},{3,387},{4,132},{5,389},{6,134},{7,391},{8... | collective-permute-start | bytes 3145736 | tf_op jit(solution)/shard_map/ppermute | solution.py:37
  86.3 0.0 collective-permute-done.11
  86.3 4.5 %collective-permute-start.14 = (bf16[128,4096]{1,0:T(8,128)(2,1)S(1)}, bf16[128,4096]{1,0:T(8,128)(2,1)S(1)}, u32[]{:S(2)}, u32[]{:S(2)}) collective-permute-start(bf16[128,4096]{1,0:T(8,128)(2,1)S(1)} %constant_dynamic-update-slice_fusion), channel_id=1, source_target_pairs={{0,2},{1,7},{2,4},{3,1},{4,6},{5,3},{6,0},{7,5},{8,10},{9,15},{10,... | collective-permute-start | bytes 3145736 | tf_op jit(solution)/shard_map/ppermute | solution.py:37
  90.8 0.8 constant_dynamic-update-slice_fusion.6
  91.7 0.0 collective-permute-done.12
  91.7 10.1 %collective-permute-start.15 = (bf16[128,4096]{1,0:T(8,128)(2,1)S(1)}, bf16[128,4096]{1,0:T(8,128)(2,1)S(1)}, u32[]{:S(2)}, u32[]{:S(2)}) collective-permute-start(bf16[128,4096]{1,0:T(8,128)(2,1)S(1)} %constant_dynamic-update-slice_fusion), channel_id=1, source_target_pairs={{0,8},{1,121},{2,10},{3,123},{4,12},{5,125},{6,14},{7,127},{8,16},... | collective-permute-start | bytes 3145736 | tf_op jit(solution)/shard_map/ppermute | solution.py:37
  101.7 0.8 constant_dynamic-update-slice_fusion.5
  102.6 0.0 collective-permute-done.10
  102.6 1.9 %collective-permute-start.16 = (bf16[128,4096]{1,0:T(8,128)(2,1)}, bf16[128,4096]{1,0:T(8,128)(2,1)}, u32[]{:S(2)}, u32[]{:S(2)}) collective-permute-start(bf16[128,4096]{1,0:T(8,128)(2,1)} %constant_dynamic-update-slice_fusion.5), channel_id=1, source_target_pairs={{0,128},{1,385},{2,130},{3,387},{4,132},{5,389},{6,134},{7,391},{8... | collective-permute-start | bytes 3145736 | tf_op jit(solution)/shard_map/ppermute | solution.py:37
  104.5 0.8 convolution_convert_fusion.7.refs_0_
  105.3 2.0 %convolution_convert_fusion.6.refs_1_ = bf16[128,512]{1,0:T(8,128)(2,1)S(1)} fusion(bf16[128,4096]{1,0:T(8,128)(2,1)} %constant_dynamic-update-slice_fusion.5, bf16[4096,256]{1,0:T(8,128)(2,1)S(1)} %collective-permute-done.10, bf16[4096,128]{1,0:T(8,128)(2,1)S(1)} %bitcast.19, bf16[4096,128]{1,0:T(8,128)(2,1)S(1)} %bitcast.28), kind=kOutput, calls=%fused_computation.13 | convolution fusion | flops 549519360 | bytes 5373952 | tf_op jit(solution)/shard_map/dot_general | solution.py:163
  107.4 0.0 collective-permute-done.13
  107.4 1.9 %collective-permute-start.17 = (bf16[128,4096]{1,0:T(8,128)(2,1)}, bf16[128,4096]{1,0:T(8,128)(2,1)}, u32[]{:S(2)}, u32[]{:S(2)}) collective-permute-start(bf16[128,4096]{1,0:T(8,128)(2,1)} %constant_dynamic-update-slice_fusion.5), channel_id=1, source_target_pairs={{0,2},{1,7},{2,4},{3,1},{4,6},{5,3},{6,0},{7,5},{8,10},{9,15},{10,... | collective-permute-start | bytes 3145736 | tf_op jit(solution)/shard_map/ppermute | solution.py:37
  109.3 0.8 convolution_convert_fusion.5.refs_2_
  110.1 0.0 collective-permute-done.14
  110.1 4.7 %collective-permute-start.18 = (bf16[128,4096]{1,0:T(8,128)(2,1)}, bf16[128,4096]{1,0:T(8,128)(2,1)}, u32[]{:S(2)}, u32[]{:S(2)}) collective-permute-start(bf16[128,4096]{1,0:T(8,128)(2,1)} %constant_dynamic-update-slice_fusion.5), channel_id=1, source_target_pairs={{0,8},{1,121},{2,10},{3,123},{4,12},{5,125},{6,14},{7,127},{8,16},... | collective-permute-start | bytes 3145736 | tf_op jit(solution)/shard_map/ppermute | solution.py:37
  114.8 0.8 convolution_convert_fusion.4.refs_3_
  115.6 0.0 collective-permute-done.15
  115.6 0.8 convolution_convert_fusion.3.refs_4_
  116.4 0.0 collective-permute-done
  116.5 0.0 all-gather.2.cloned.1.call-done
  116.5 4.2 %fusion.4.query_ref = bf16[512,256]{1,0:T(8,128)(2,1)S(1)} fusion(bf16[512,4096]{1,0:T(8,128)(2,1)} %all-gather.2.cloned.1.call-done, bf16[4096,128]{1,0:T(8,128)(2,1)} %collective-permute-done, bf16[4096,128]{1,0:T(8,128)(2,1)} %bitcast.40), kind=kOutput, calls=%fused_computation.6 | convolution fusion | flops 1078067200 | bytes 6553600 | tf_op jit(solution)/shard_map/dot_general | solution.py:162
  120.7 2.9 %collective-permute-done.17 = bf16[128,4096]{1,0:T(8,128)(2,1)} collective-permute-done((bf16[128,4096]{1,0:T(8,128)(2,1)}, bf16[128,4096]{1,0:T(8,128)(2,1)}, u32[]{:S(2)}, u32[]{:S(2)}) %collective-permute-start.17) | collective-permute-done | bytes 1048608 | tf_op jit(solution)/shard_map/ppermute | solution.py:37
  123.5 3.3 %collective-permute-done.18 = bf16[128,4096]{1,0:T(8,128)(2,1)} collective-permute-done((bf16[128,4096]{1,0:T(8,128)(2,1)}, bf16[128,4096]{1,0:T(8,128)(2,1)}, u32[]{:S(2)}, u32[]{:S(2)}) %collective-permute-start.18) | collective-permute-done | bytes 1048608 | tf_op jit(solution)/shard_map/ppermute | solution.py:37
  126.9 2.0 %convolution_convert_fusion.2.refs_5_ = bf16[128,512]{1,0:T(8,128)(2,1)S(1)} fusion(bf16[128,4096]{1,0:T(8,128)(2,1)} %collective-permute-done.16, bf16[4096,256]{1,0:T(8,128)(2,1)S(1)} %copy-done.5, bf16[4096,128]{1,0:T(8,128)(2,1)S(1)} %bitcast.23, bf16[4096,128]{1,0:T(8,128)(2,1)S(1)} %bitcast.32), kind=kOutput, calls=%fused_computation.9 | convolution fusion | flops 549519360 | bytes 5373952 | tf_op jit(solution)/shard_map/dot_general | solution.py:163
  128.9 2.0 %convolution_convert_fusion.1.refs_6_ = bf16[128,512]{1,0:T(8,128)(2,1)S(1)} fusion(bf16[128,4096]{1,0:T(8,128)(2,1)} %collective-permute-done.17, bf16[4096,256]{1,0:T(8,128)(2,1)S(1)} %copy-done.5, bf16[4096,128]{1,0:T(8,128)(2,1)S(1)} %bitcast.24, bf16[4096,128]{1,0:T(8,128)(2,1)S(1)} %bitcast.33), kind=kOutput, calls=%fused_computation.8 | convolution fusion | flops 549519360 | bytes 5373952 | tf_op jit(solution)/shard_map/dot_general | solution.py:163
  131.0 2.0 %convolution_convert_fusion.refs_7_ = bf16[128,512]{1,0:T(8,128)(2,1)S(1)} fusion(bf16[128,4096]{1,0:T(8,128)(2,1)} %collective-permute-done.18, bf16[4096,256]{1,0:T(8,128)(2,1)S(1)} %copy-done.5, bf16[4096,128]{1,0:T(8,128)(2,1)S(1)} %bitcast.25, bf16[4096,128]{1,0:T(8,128)(2,1)S(1)} %bitcast.34), kind=kOutput, calls=%fused_computation.7 | convolution fusion | flops 549519360 | bytes 5373952 | tf_op jit(solution)/shard_map/dot_general | solution.py:163
  133.0 3.5 %shard_map.65 = (f32[512,256]{1,0:T(8,128)S(1)}, f32[512,256]{1,0:T(8,128)S(1)}) custom-call(bf16[512,256]{1,0:T(8,128)(2,1)S(1)} %fusion.4.query_ref, bf16[128,512]{1,0:T(8,128)(2,1)S(1)} %convolution_convert_fusion.7.refs_0_, bf16[128,512]{1,0:T(8,128)(2,1)S(1)} %convolution_convert_fusion.6.refs_1_, ...), custom_call_target="tpu_custom_call" | custom-call | flops 536870912 | bytes 2359296 | tf_op jit(solution)/shard_map/pallas_call | solution.py:117
  136.5 8.3 %collective-permute-start.19 = (f32[512,256]{1,0:T(8,128)S(1)}, f32[512,256]{1,0:T(8,128)S(1)}, u32[]{:S(2)}, u32[]{:S(2)}) collective-permute-start(f32[512,256]{1,0:T(8,128)S(1)} %get-tuple-element.18), channel_id=1, source_target_pairs={{0,1},{1,0},{2,3},{3,2},{4,5},{5,4},{6,7},{7,6},{8,9},{9,8},{10,11... | collective-permute-start | bytes 1572872 | tf_op jit(solution)/shard_map/ppermute | solution.py:37
  144.8 1.5 collective-permute-done.19
  146.3 0.5 fusion.15
  146.8 0.3 fusion.13
  147.1 13.4 %all_to_all.5 = bf16[32,16,128]{2,1,0:T(8,128)(2,1)S(1)} all-to-all(bf16[32,16,128]{2,1,0:T(8,128)(2,1)S(1)} %bitcast.35), channel_id=1, replica_groups=mesh['x'=4,'zh'=4,'zl'=4,'y'=4,'core'=2] {'zl','y','core'}, dimensions={0} | all-to-all | bytes 262144 | tf_op jit(solution)/shard_map/all_to_all | solution.py:179
  160.5 0.7 reshape.7
  (19 shorter events, 0.2 us)
Async XLA Ops:
  6.5 109.9 %all-gather.2.cloned.1.call-start = ((), (), s32[]{:S(2)}) async-start(), calls=%async_computation.1 | async-start | bytes 4325376 | tf_op jit(solution)/shard_map/all_gather | solution.py:144
  6.5 0.9 copy-start
  7.4 0.7 copy-start.1
  10.0 7.9 %collective-permute-start.1 = (bf16[16,4096]{1,0:T(8,128)(2,1)S(1)}, bf16[16,4096]{1,0:T(8,128)(2,1)S(1)}, u32[]{:S(2)}, u32[]{:S(2)}) collective-permute-start(bf16[16,4096]{1,0:T(8,128)(2,1)S(1)} %get-tuple-element.26), channel_id=1, source_target_pairs={{0,384},{1,385},{2,386},{3,387},{4,388},{5,389},{6,390},{7,391},{8... | collective-permute-start | bytes 393224 | tf_op jit(solution)/shard_map/ppermute | solution.py:37
  15.2 3.2 %collective-permute-start.2 = (bf16[16,4096]{1,0:T(8,128)(2,1)S(1)}, bf16[16,4096]{1,0:T(8,128)(2,1)S(1)}, u32[]{:S(2)}, u32[]{:S(2)}) collective-permute-start(bf16[16,4096]{1,0:T(8,128)(2,1)S(1)} %get-tuple-element.25), channel_id=1, source_target_pairs={{0,128},{1,129},{2,130},{3,131},{4,132},{5,133},{6,134},{7,135},{8... | collective-permute-start | bytes 393224 | tf_op jit(solution)/shard_map/ppermute | solution.py:37
  16.6 3.3 %collective-permute-start.3 = (bf16[16,4096]{1,0:T(8,128)(2,1)S(1)}, bf16[16,4096]{1,0:T(8,128)(2,1)S(1)}, u32[]{:S(2)}, u32[]{:S(2)}) collective-permute-start(bf16[16,4096]{1,0:T(8,128)(2,1)S(1)} %get-tuple-element.24), channel_id=1, source_target_pairs={{0,256},{1,257},{2,258},{3,259},{4,260},{5,261},{6,262},{7,263},{8... | collective-permute-start | bytes 393224 | tf_op jit(solution)/shard_map/ppermute | solution.py:37
  20.8 13.7 %collective-permute-start.4 = (bf16[16,4096]{1,0:T(8,128)(2,1)S(1)}, bf16[16,4096]{1,0:T(8,128)(2,1)S(1)}, u32[]{:S(2)}, u32[]{:S(2)}) collective-permute-start(bf16[16,4096]{1,0:T(8,128)(2,1)S(1)} %select_select_fusion), channel_id=1, source_target_pairs={{0,32},{1,97},{2,34},{3,99},{4,36},{5,101},{6,38},{7,103},{8,40},{... | collective-permute-start | bytes 393224 | tf_op jit(solution)/shard_map/ppermute | solution.py:37
  34.5 3.6 %collective-permute-start.5 = (bf16[16,4096]{1,0:T(8,128)(2,1)S(1)}, bf16[16,4096]{1,0:T(8,128)(2,1)S(1)}, u32[]{:S(2)}, u32[]{:S(2)}) collective-permute-start(bf16[16,4096]{1,0:T(8,128)(2,1)S(1)} %broadcast_select_fusion), channel_id=1, source_target_pairs={{0,96},{1,33},{2,98},{3,35},{4,100},{5,37},{6,102},{7,39},{8,104},... | collective-permute-start | bytes 393224 | tf_op jit(solution)/shard_map/ppermute | solution.py:37
  35.8 80.6 %collective-permute-start = (bf16[4096,128]{1,0:T(8,128)(2,1)}, bf16[4096,128]{1,0:T(8,128)(2,1)}, u32[]{:S(2)}, u32[]{:S(2)}) collective-permute-start(bf16[4096,128]{1,0:T(8,128)(2,1)} %bitcast.39), channel_id=1, source_target_pairs={{0,1},{1,0},{2,3},{3,2},{4,5},{5,4},{6,7},{7,6},{8,9},{9,8},{10,11... | collective-permute-start | bytes 3145736 | tf_op jit(solution)/shard_map/ppermute | solution.py:37
  38.2 23.7 %collective-permute-start.6 = (bf16[16,4096]{1,0:T(8,128)(2,1)S(1)}, bf16[16,4096]{1,0:T(8,128)(2,1)S(1)}, u32[]{:S(2)}, u32[]{:S(2)}) collective-permute-start(bf16[16,4096]{1,0:T(8,128)(2,1)S(1)} %get-tuple-element.23), channel_id=1, source_target_pairs={{0,276},{1,373},{2,278},{3,375},{4,272},{5,369},{6,274},{7,371},{8... | collective-permute-start | bytes 393224 | tf_op jit(solution)/shard_map/ppermute | solution.py:37
  48.4 13.5 %collective-permute-start.7 = (bf16[16,4096]{1,0:T(8,128)(2,1)S(1)}, bf16[16,4096]{1,0:T(8,128)(2,1)S(1)}, u32[]{:S(2)}, u32[]{:S(2)}) collective-permute-start(bf16[16,4096]{1,0:T(8,128)(2,1)S(1)} %get-tuple-element.23), channel_id=1, source_target_pairs={{0,250},{1,399},{2,252},{3,393},{4,254},{5,395},{6,248},{7,397},{8... | collective-permute-start | bytes 393224 | tf_op jit(solution)/shard_map/ppermute | solution.py:37
  51.7 10.2 %collective-permute-start.8 = (bf16[16,4096]{1,0:T(8,128)(2,1)S(1)}, bf16[16,4096]{1,0:T(8,128)(2,1)S(1)}, u32[]{:S(2)}, u32[]{:S(2)}) collective-permute-start(bf16[16,4096]{1,0:T(8,128)(2,1)S(1)} %get-tuple-element.23), channel_id=1, source_target_pairs={{0,398},{1,251},{2,392},{3,253},{4,394},{5,255},{6,396},{7,249},{8... | collective-permute-start | bytes 393224 | tf_op jit(solution)/shard_map/ppermute | solution.py:37
  58.0 46.5 %copy-start.2 = (bf16[1,4096,128]{2,1,0:T(8,128)(2,1)S(1)}, bf16[1,4096,128]{2,1,0:T(8,128)(2,1)}, u32[]{:S(2)}) copy-start(bf16[1,4096,128]{2,1,0:T(8,128)(2,1)} %param.11) | copy-start | bytes 3145732
  58.0 46.5 %copy-start.3 = (bf16[1,4096,128]{2,1,0:T(8,128)(2,1)S(1)}, bf16[1,4096,128]{2,1,0:T(8,128)(2,1)}, u32[]{:S(2)}) copy-start(bf16[1,4096,128]{2,1,0:T(8,128)(2,1)} %param.10) | copy-start | bytes 3145732
  60.0 42.6 %collective-permute-start.10 = (bf16[4096,256]{1,0:T(8,128)(2,1)S(1)}, bf16[4096,256]{1,0:T(8,128)(2,1)S(1)}, u32[]{:S(2)}, u32[]{:S(2)}) collective-permute-start(bf16[4096,256]{1,0:T(8,128)(2,1)S(1)} %pad_maximum_fusion.1), channel_id=1, source_target_pairs={{0,1},{1,0},{2,3},{3,2},{4,5},{5,4},{6,7},{7,6},{8,9},{9,8},{10,11... | collective-permute-start | bytes 6291464 | tf_op jit(solution)/shard_map/ppermute | solution.py:37
  62.0 20.5 %collective-permute-start.9 = (bf16[64,4096]{1,0:T(8,128)(2,1)S(1)}, bf16[64,4096]{1,0:T(8,128)(2,1)S(1)}, u32[]{:S(2)}, u32[]{:S(2)}) collective-permute-start(bf16[64,4096]{1,0:T(8,128)(2,1)S(1)} %pad_maximum_fusion.2), channel_id=1, source_target_pairs={{0,136},{1,505},{2,138},{3,507},{4,140},{5,509},{6,142},{7,511},{8... | collective-permute-start | bytes 1572872 | tf_op jit(solution)/shard_map/ppermute | solution.py:37
  65.8 20.6 %collective-permute-start.11 = (bf16[64,4096]{1,0:T(8,128)(2,1)S(1)}, bf16[64,4096]{1,0:T(8,128)(2,1)S(1)}, u32[]{:S(2)}, u32[]{:S(2)}) collective-permute-start(bf16[64,4096]{1,0:T(8,128)(2,1)S(1)} %pad_maximum_fusion.2), channel_id=1, source_target_pairs={{0,504},{1,137},{2,506},{3,139},{4,508},{5,141},{6,510},{7,143},{8... | collective-permute-start | bytes 1572872 | tf_op jit(solution)/shard_map/ppermute | solution.py:37
  68.2 23.5 %collective-permute-start.12 = (bf16[64,4096]{1,0:T(8,128)(2,1)S(1)}, bf16[64,4096]{1,0:T(8,128)(2,1)S(1)}, u32[]{:S(2)}, u32[]{:S(2)}) collective-permute-start(bf16[64,4096]{1,0:T(8,128)(2,1)S(1)} %pad_maximum_fusion.2), channel_id=1, source_target_pairs={{0,4},{1,5},{2,6},{3,7},{4,0},{5,1},{6,2},{7,3},{8,12},{9,13},{10,... | collective-permute-start | bytes 1572872 | tf_op jit(solution)/shard_map/ppermute | solution.py:37
  82.5 24.9 %collective-permute-start.13 = (bf16[128,4096]{1,0:T(8,128)(2,1)S(1)}, bf16[128,4096]{1,0:T(8,128)(2,1)S(1)}, u32[]{:S(2)}, u32[]{:S(2)}) collective-permute-start(bf16[128,4096]{1,0:T(8,128)(2,1)S(1)} %constant_dynamic-update-slice_fusion), channel_id=1, source_target_pairs={{0,128},{1,385},{2,130},{3,387},{4,132},{5,389},{6,134},{7,391},{8... | collective-permute-start | bytes 3145736 | tf_op jit(solution)/shard_map/ppermute | solution.py:37
  86.3 23.8 %collective-permute-start.14 = (bf16[128,4096]{1,0:T(8,128)(2,1)S(1)}, bf16[128,4096]{1,0:T(8,128)(2,1)S(1)}, u32[]{:S(2)}, u32[]{:S(2)}) collective-permute-start(bf16[128,4096]{1,0:T(8,128)(2,1)S(1)} %constant_dynamic-update-slice_fusion), channel_id=1, source_target_pairs={{0,2},{1,7},{2,4},{3,1},{4,6},{5,3},{6,0},{7,5},{8,10},{9,15},{10,... | collective-permute-start | bytes 3145736 | tf_op jit(solution)/shard_map/ppermute | solution.py:37
  91.7 23.9 %collective-permute-start.15 = (bf16[128,4096]{1,0:T(8,128)(2,1)S(1)}, bf16[128,4096]{1,0:T(8,128)(2,1)S(1)}, u32[]{:S(2)}, u32[]{:S(2)}) collective-permute-start(bf16[128,4096]{1,0:T(8,128)(2,1)S(1)} %constant_dynamic-update-slice_fusion), channel_id=1, source_target_pairs={{0,8},{1,121},{2,10},{3,123},{4,12},{5,125},{6,14},{7,127},{8,16},... | collective-permute-start | bytes 3145736 | tf_op jit(solution)/shard_map/ppermute | solution.py:37
  102.6 13.1 %copy-start.4 = (bf16[4096,256]{1,0:T(8,128)(2,1)}, bf16[4096,256]{1,0:T(8,128)(2,1)S(1)}, u32[]{:S(2)}) copy-start(bf16[4096,256]{1,0:T(8,128)(2,1)S(1)} %collective-permute-done.10) | copy-start | bytes 6291460
  102.6 18.1 %collective-permute-start.16 = (bf16[128,4096]{1,0:T(8,128)(2,1)}, bf16[128,4096]{1,0:T(8,128)(2,1)}, u32[]{:S(2)}, u32[]{:S(2)}) collective-permute-start(bf16[128,4096]{1,0:T(8,128)(2,1)} %constant_dynamic-update-slice_fusion.5), channel_id=1, source_target_pairs={{0,128},{1,385},{2,130},{3,387},{4,132},{5,389},{6,134},{7,391},{8... | collective-permute-start | bytes 3145736 | tf_op jit(solution)/shard_map/ppermute | solution.py:37
  107.4 16.2 %collective-permute-start.17 = (bf16[128,4096]{1,0:T(8,128)(2,1)}, bf16[128,4096]{1,0:T(8,128)(2,1)}, u32[]{:S(2)}, u32[]{:S(2)}) collective-permute-start(bf16[128,4096]{1,0:T(8,128)(2,1)} %constant_dynamic-update-slice_fusion.5), channel_id=1, source_target_pairs={{0,2},{1,7},{2,4},{3,1},{4,6},{5,3},{6,0},{7,5},{8,10},{9,15},{10,... | collective-permute-start | bytes 3145736 | tf_op jit(solution)/shard_map/ppermute | solution.py:37
  110.1 16.7 %collective-permute-start.18 = (bf16[128,4096]{1,0:T(8,128)(2,1)}, bf16[128,4096]{1,0:T(8,128)(2,1)}, u32[]{:S(2)}, u32[]{:S(2)}) collective-permute-start(bf16[128,4096]{1,0:T(8,128)(2,1)} %constant_dynamic-update-slice_fusion.5), channel_id=1, source_target_pairs={{0,8},{1,121},{2,10},{3,123},{4,12},{5,125},{6,14},{7,127},{8,16},... | collective-permute-start | bytes 3145736 | tf_op jit(solution)/shard_map/ppermute | solution.py:37
  116.5 10.4 %copy-start.5 = (bf16[4096,256]{1,0:T(8,128)(2,1)S(1)}, bf16[4096,256]{1,0:T(8,128)(2,1)}, u32[]{:S(2)}) copy-start(bf16[4096,256]{1,0:T(8,128)(2,1)} %copy-done.4) | copy-start | bytes 6291460
  136.5 9.8 %collective-permute-start.19 = (f32[512,256]{1,0:T(8,128)S(1)}, f32[512,256]{1,0:T(8,128)S(1)}, u32[]{:S(2)}, u32[]{:S(2)}) collective-permute-start(f32[512,256]{1,0:T(8,128)S(1)} %get-tuple-element.18), channel_id=1, source_target_pairs={{0,1},{1,0},{2,3},{3,2},{4,5},{5,4},{6,7},{7,6},{8,9},{9,8},{10,11... | collective-permute-start | bytes 1572872 | tf_op jit(solution)/shard_map/ppermute | solution.py:37
Sparse Core Ops, SparseCore 0:
  18.0 80.0 all-gather.1

commit v4 on v2

--- a/solution.py
+++ b/solution.py
@@ -120,7 +120,7 @@
         grid=(count // block,),
         in_specs=[row_spec] + [pl.BlockSpec(kv.shape, lambda i: (0, 0)) for kv in key_values],
         out_specs=(row_spec, row_spec),
-        compiler_params=pltpu.CompilerParams(vmem_limit_bytes=40 * 2**20),
+        compiler_params=pltpu.CompilerParams(vmem_limit_bytes=16 * 2**20),
         cost_estimate=pl.CostEstimate(
             flops=4 * count * keys * HD,
             bytes_accessed=keys * HD * 4 + count * HD * 10,
@@ -136,7 +136,9 @@
     half = HD // 2
 
     normed = pl.pallas_call(
-        norm_kernel, out_shape=jax.ShapeDtypeStruct(dec_states.shape[1:], jnp.bfloat16)
+        norm_kernel,
+        out_shape=jax.ShapeDtypeStruct(dec_states.shape[1:], jnp.bfloat16),
+        compiler_params=pltpu.CompilerParams(vmem_limit_bytes=4 * 2**20),
     )(dec_states[0], norm_gain)
     encoder_rows, normed = lax.optimization_barrier((section_states[0], normed))
     normed_all = lax.all_gather(normed, SEQ, axis=0, tiled=True)
@@ -145,12 +147,12 @@
 
     other_core = pairs_of(lambda x, zh, zl, y, c: (x, zh, zl, y, 1 - c))
     kv_mine = jnp.concatenate([w_key[0], w_value[0]], axis=1)
-    piece, kv_mine, query_mine = lax.optimization_barrier((piece, kv_mine, w_query[0]))
+    query_mine = w_query[0]
     kv_other, query_other = send(kv_mine, other_core), send(query_mine, other_core)
     piece = spread_z(piece)
-    piece, kv_other, query_other = lax.optimization_barrier((piece, kv_other, query_other))
 
-    piece = jnp.concatenate(widen(piece, ((2, 2, 2), (1, 1, -1), (-1, -1, 1))), axis=0)
+    piece = jnp.concatenate(widen(piece, ((2, 2, 2),)), axis=0)
+    piece = jnp.concatenate(widen(piece, ((1, 1, -1),)), axis=0)
     quarter = jnp.concatenate(widen(piece, ((1, 0, 1), (-1, 0, -1), (0, 2, 0))), axis=0)
     _, *arrived = widen(quarter, ((1, 0, 0), (0, 1, 0), (0, 0, 1)))
 
@@ -159,7 +161,7 @@
     queries = jnp.dot(normed_all, query_cols, preferred_element_type=jnp.float32).astype(jnp.bfloat16)
     project = lambda rows: jnp.dot(rows, kv_cols, preferred_element_type=jnp.float32).astype(jnp.bfloat16)
     near = project(quarter)
-    queries, near, *arrived = lax.optimization_barrier((queries, near, *arrived))
+    queries, near, arrived[0] = lax.optimization_barrier((queries, near, arrived[0]))
     key_values = [near] + [project(rows) for rows in arrived]
 
     own, outgoing = attend(queries, key_values)

time: 168 us -> 165 us (0.982)
  waiting for transfers between devices: 40.5 us -> 48.8 us
  starting transfers between devices: 66.1 us -> 59.6 us
  local copies, waits for them, and re-layouts: 10.9 us -> 7.39 us
    ppermute x17 -> x16, waiting for transfers between devices: 40.4 us -> 48.8 us  [send(): return lax.ppermute(value, AXES, pairs)]
    ppermute x17 -> x16, starting transfers between devices: 66.1 us -> 59.6 us  [send(): return lax.ppermute(value, AXES, pairs)]
    concatenate x2 -> x0, local copies, waits for them, and re-layouts: 2.42 us -> none  [the longest x1 1.75 us: local(): kv_cols = jnp.concatenate([kv_mine, kv_other], axis=1)]
    unnamed x12 -> x18, local copies, waits for them, and re-layouts: 5.83 us -> 4.73 us
  transfers between devices with their start and end apart: 18 -> 17, of which waited for: 10 -> 11; matrix products, arithmetic and copies ran while one was open for 10% -> 12% of each run, Pallas kernels for 0% -> 0%
where the time goes in v4:
time: 165 us
  starting transfers between devices  59.6 us (36%)
  waiting for transfers between devices  48.8 us (30%)
  matrix products  15.5 us (9%)
  between operations  13.8 us (8%)
  blocking collectives  11.8 us (7%)
  local copies, waits for them, and re-layouts  7.39 us (4%)
  other arithmetic  4.36 us (3%)
  Pallas kernels  3.62 us (2%)
    ppermute x16, starting transfers between devices, send(): return lax.ppermute(value, AXES, pairs)  59.6 us
    ppermute x16, waiting for transfers between devices, send(): return lax.ppermute(value, AXES, pairs)  48.8 us
    all_to_all x1, blocking collectives, local(): lax.all_to_all(parts, SEQ, split_axis=0, concat_axis=0, tiled=True)  11.8 us
    dot_general x4, matrix products, local(): jnp.dot(rows, kv_cols, preferred_element_type=jnp.float32)  11.3 us
    unnamed x18, local copies, waits for them, and re-layouts  4.73 us
    dot_general x1, matrix products, local(): jnp.dot(normed_all, query_cols, preferred_element_type=jnp.float32)  4.18 us
  transfers between devices with their start and end apart: 17, of which 11 were waited for; matrix products, arithmetic and copies ran while one was open for 12% of the time, Pallas kernels for 0%

profile of v4, /device:TPU:1, one launch (start us, length us, event | category | flops | bytes accessed | tf_op | source)
XLA Modules:
  0.0 164.8 jit_solution(8908514404621584088)
XLA Ops:
  6.5 0.0 all-gather.2.cloned.1.call-start
  6.5 0.9 copy-done
  7.4 0.7 copy-done.1
  8.2 0.8 shard_map.64
  9.0 1.1 fusion.17
  10.0 5.5 %collective-permute-start.3 = (bf16[16,4096]{1,0:T(8,128)(2,1)S(1)}, bf16[16,4096]{1,0:T(8,128)(2,1)S(1)}, u32[]{:S(2)}, u32[]{:S(2)}) collective-permute-start(bf16[16,4096]{1,0:T(8,128)(2,1)S(1)} %get-tuple-element.24), channel_id=1, source_target_pairs={{0,256},{1,257},{2,258},{3,259},{4,260},{5,261},{6,262},{7,263},{8... | collective-permute-start | bytes 393224 | tf_op jit(solution)/shard_map/ppermute | solution.py:37
  15.5 1.3 collective-permute-start.2
  16.8 1.3 collective-permute-start.1
  18.1 0.0 collective-permute-done.3
  18.1 0.7 collective-permute-done.2
  18.8 1.2 collective-permute-done.1
  20.0 0.9 select_select_fusion
  21.0 5.3 %collective-permute-start.4 = (bf16[16,4096]{1,0:T(8,128)(2,1)S(1)}, bf16[16,4096]{1,0:T(8,128)(2,1)S(1)}, u32[]{:S(2)}, u32[]{:S(2)}) collective-permute-start(bf16[16,4096]{1,0:T(8,128)(2,1)S(1)} %select_select_fusion), channel_id=1, source_target_pairs={{0,32},{1,97},{2,34},{3,99},{4,36},{5,101},{6,38},{7,103},{8,40},{... | collective-permute-start | bytes 393224 | tf_op jit(solution)/shard_map/ppermute | solution.py:37
  26.3 0.0 all-gather.2.cloned.1.call-update
  26.4 9.6 %collective-permute-done.4 = bf16[16,4096]{1,0:T(8,128)(2,1)S(1)} collective-permute-done((bf16[16,4096]{1,0:T(8,128)(2,1)S(1)}, bf16[16,4096]{1,0:T(8,128)(2,1)S(1)}, u32[]{:S(2)}, u32[]{:S(2)}) %collective-permute-start.4) | collective-permute-done | bytes 131104 | tf_op jit(solution)/shard_map/ppermute | solution.py:37
  35.9 1.3 collective-permute-start.5
  37.3 3.0 %collective-permute-done.5 = bf16[16,4096]{1,0:T(8,128)(2,1)S(1)} collective-permute-done((bf16[16,4096]{1,0:T(8,128)(2,1)S(1)}, bf16[16,4096]{1,0:T(8,128)(2,1)S(1)}, u32[]{:S(2)}, u32[]{:S(2)}) %collective-permute-start.5) | collective-permute-done | bytes 131104 | tf_op jit(solution)/shard_map/ppermute | solution.py:37
  40.2 0.7 constant_dynamic-update-slice_fusion.5
  40.9 4.8 %collective-permute-start.6 = (bf16[16,4096]{1,0:T(8,128)(2,1)S(1)}, bf16[16,4096]{1,0:T(8,128)(2,1)S(1)}, u32[]{:S(2)}, u32[]{:S(2)}) collective-permute-start(bf16[16,4096]{1,0:T(8,128)(2,1)S(1)} %get-tuple-element.23), channel_id=1, source_target_pairs={{0,276},{1,373},{2,278},{3,375},{4,272},{5,369},{6,274},{7,371},{8... | collective-permute-start | bytes 393224 | tf_op jit(solution)/shard_map/ppermute | solution.py:37
  45.7 6.8 %collective-permute-done.6 = bf16[16,4096]{1,0:T(8,128)(2,1)S(1)} collective-permute-done((bf16[16,4096]{1,0:T(8,128)(2,1)S(1)}, bf16[16,4096]{1,0:T(8,128)(2,1)S(1)}, u32[]{:S(2)}, u32[]{:S(2)}) %collective-permute-start.6) | collective-permute-done | bytes 131104 | tf_op jit(solution)/shard_map/ppermute | solution.py:37
  52.5 3.3 %collective-permute-start.7 = (bf16[32,4096]{1,0:T(8,128)(2,1)S(1)}, bf16[32,4096]{1,0:T(8,128)(2,1)S(1)}, u32[]{:S(2)}, u32[]{:S(2)}) collective-permute-start(bf16[32,4096]{1,0:T(8,128)(2,1)S(1)} %pad_maximum_fusion.3), channel_id=1, source_target_pairs={{0,250},{1,399},{2,252},{3,393},{4,254},{5,395},{6,248},{7,397},{8... | collective-permute-start | bytes 786440 | tf_op jit(solution)/shard_map/ppermute | solution.py:37
  55.8 0.0 copy-start.6
  55.8 0.0 copy-start.2
  55.8 0.0 copy-start.3
  55.8 1.9 %pad_maximum_fusion.1 = bf16[4096,256]{1,0:T(8,128)(2,1)S(1)} fusion(bf16[4096,128]{1,0:T(8,128)(2,1)} %bitcast.13, bf16[4096,128]{1,0:T(8,128)(2,1)} %bitcast.18), kind=kLoop, calls=%fused_computation.5 | loop fusion | flops 4194304 | bytes 4194304 | tf_op jit(solution)/shard_map/concatenate | solution.py:149
  57.7 9.8 %collective-permute-start.11 = (bf16[4096,256]{1,0:T(8,128)(2,1)S(1)}, bf16[4096,256]{1,0:T(8,128)(2,1)S(1)}, u32[]{:S(2)}, u32[]{:S(2)}) collective-permute-start(bf16[4096,256]{1,0:T(8,128)(2,1)S(1)} %pad_maximum_fusion.1), channel_id=1, source_target_pairs={{0,1},{1,0},{2,3},{3,2},{4,5},{5,4},{6,7},{7,6},{8,9},{9,8},{10,11... | collective-permute-start | bytes 6291464 | tf_op jit(solution)/shard_map/ppermute | solution.py:37
  67.6 0.0 collective-permute-done.7
  67.6 2.0 %collective-permute-start.8 = (bf16[64,4096]{1,0:T(8,128)(2,1)S(1)}, bf16[64,4096]{1,0:T(8,128)(2,1)S(1)}, u32[]{:S(2)}, u32[]{:S(2)}) collective-permute-start(bf16[64,4096]{1,0:T(8,128)(2,1)S(1)} %pad_maximum_fusion.2), channel_id=1, source_target_pairs={{0,136},{1,505},{2,138},{3,507},{4,140},{5,509},{6,142},{7,511},{8... | collective-permute-start | bytes 1572872 | tf_op jit(solution)/shard_map/ppermute | solution.py:37
  69.7 0.7 constant_dynamic-update-slice_fusion.4
  70.3 9.0 %collective-permute-start.10 = (bf16[64,4096]{1,0:T(8,128)(2,1)S(1)}, bf16[64,4096]{1,0:T(8,128)(2,1)S(1)}, u32[]{:S(2)}, u32[]{:S(2)}) collective-permute-start(bf16[64,4096]{1,0:T(8,128)(2,1)S(1)} %pad_maximum_fusion.2), channel_id=1, source_target_pairs={{0,4},{1,5},{2,6},{3,7},{4,0},{5,1},{6,2},{7,3},{8,12},{9,13},{10,... | collective-permute-start | bytes 1572872 | tf_op jit(solution)/shard_map/ppermute | solution.py:37
  79.4 1.9 %collective-permute-start.9 = (bf16[64,4096]{1,0:T(8,128)(2,1)S(1)}, bf16[64,4096]{1,0:T(8,128)(2,1)S(1)}, u32[]{:S(2)}, u32[]{:S(2)}) collective-permute-start(bf16[64,4096]{1,0:T(8,128)(2,1)S(1)} %pad_maximum_fusion.2), channel_id=1, source_target_pairs={{0,504},{1,137},{2,506},{3,139},{4,508},{5,141},{6,510},{7,143},{8... | collective-permute-start | bytes 1572872 | tf_op jit(solution)/shard_map/ppermute | solution.py:37
  81.3 0.7 constant_dynamic-update-slice_fusion.3
  82.0 1.9 %collective-permute-done.8 = bf16[64,4096]{1,0:T(8,128)(2,1)S(1)} collective-permute-done((bf16[64,4096]{1,0:T(8,128)(2,1)S(1)}, bf16[64,4096]{1,0:T(8,128)(2,1)S(1)}, u32[]{:S(2)}, u32[]{:S(2)}) %collective-permute-start.8) | collective-permute-done | bytes 524320 | tf_op jit(solution)/shard_map/ppermute | solution.py:37
  83.9 0.9 constant_dynamic-update-slice_fusion.2
  84.8 7.8 %collective-permute-done.9 = bf16[64,4096]{1,0:T(8,128)(2,1)S(1)} collective-permute-done((bf16[64,4096]{1,0:T(8,128)(2,1)S(1)}, bf16[64,4096]{1,0:T(8,128)(2,1)S(1)}, u32[]{:S(2)}, u32[]{:S(2)}) %collective-permute-start.9) | collective-permute-done | bytes 524320 | tf_op jit(solution)/shard_map/ppermute | solution.py:37
  92.6 0.8 constant_dynamic-update-slice_fusion.1
  93.4 0.4 collective-permute-done.10
  93.8 0.9 constant_dynamic-update-slice_fusion
  94.7 6.4 %collective-permute-start.14 = (bf16[256,4096]{1,0:T(8,128)(2,1)}, bf16[256,4096]{1,0:T(8,128)(2,1)S(1)}, u32[]{:S(2)}, u32[]{:S(2)}) collective-permute-start(bf16[256,4096]{1,0:T(8,128)(2,1)} %constant_dynamic-update-slice_fusion), channel_id=1, source_target_pairs={{0,8},{1,121},{2,10},{3,123},{4,12},{5,125},{6,14},{7,127},{8,16},... | collective-permute-start | bytes 6291464 | tf_op jit(solution)/shard_map/ppermute | solution.py:37
  101.1 1.9 %collective-permute-start.13 = (bf16[256,4096]{1,0:T(8,128)(2,1)}, bf16[256,4096]{1,0:T(8,128)(2,1)S(1)}, u32[]{:S(2)}, u32[]{:S(2)}) collective-permute-start(bf16[256,4096]{1,0:T(8,128)(2,1)} %constant_dynamic-update-slice_fusion), channel_id=1, source_target_pairs={{0,2},{1,7},{2,4},{3,1},{4,6},{5,3},{6,0},{7,5},{8,10},{9,15},{10,... | collective-permute-start | bytes 6291464 | tf_op jit(solution)/shard_map/ppermute | solution.py:37
  103.0 0.0 copy-done.6
  103.0 1.9 %collective-permute-start = (bf16[4096,128]{1,0:T(8,128)(2,1)S(1)}, bf16[4096,128]{1,0:T(8,128)(2,1)}, u32[]{:S(2)}, u32[]{:S(2)}) collective-permute-start(bf16[4096,128]{1,0:T(8,128)(2,1)S(1)} %bitcast.28), channel_id=1, source_target_pairs={{0,1},{1,0},{2,3},{3,2},{4,5},{5,4},{6,7},{7,6},{8,9},{9,8},{10,11... | collective-permute-start | bytes 3145736 | tf_op jit(solution)/shard_map/ppermute | solution.py:37
  105.0 1.9 %collective-permute-start.12 = (bf16[256,4096]{1,0:T(8,128)(2,1)}, bf16[256,4096]{1,0:T(8,128)(2,1)}, u32[]{:S(2)}, u32[]{:S(2)}) collective-permute-start(bf16[256,4096]{1,0:T(8,128)(2,1)} %constant_dynamic-update-slice_fusion), channel_id=1, source_target_pairs={{0,128},{1,385},{2,130},{3,387},{4,132},{5,389},{6,134},{7,391},{8... | collective-permute-start | bytes 6291464 | tf_op jit(solution)/shard_map/ppermute | solution.py:37
  106.9 0.0 collective-permute-done.11
  106.9 0.0 copy-done.2
  106.9 0.0 copy-done.3
  106.9 0.0 copy-start.4
  106.9 3.6 %convolution_convert_fusion.3.refs_0_ = bf16[256,512]{1,0:T(8,128)(2,1)S(1)} fusion(bf16[256,4096]{1,0:T(8,128)(2,1)} %constant_dynamic-update-slice_fusion, bf16[4096,256]{1,0:T(8,128)(2,1)S(1)} %collective-permute-done.11, bf16[4096,128]{1,0:T(8,128)(2,1)S(1)} %bitcast.14, bf16[4096,128]{1,0:T(8,128)(2,1)S(1)} %bitcast.19), kind=kOutput, calls=%fused_computation.10 | convolution fusion | flops 1086455808 | bytes 6553600 | tf_op jit(solution)/shard_map/dot_general | solution.py:162
  110.6 13.8 %collective-permute-done.14 = bf16[256,4096]{1,0:T(8,128)(2,1)S(1)} collective-permute-done((bf16[256,4096]{1,0:T(8,128)(2,1)}, bf16[256,4096]{1,0:T(8,128)(2,1)S(1)}, u32[]{:S(2)}, u32[]{:S(2)}) %collective-permute-start.14) | collective-permute-done | bytes 2097184 | tf_op jit(solution)/shard_map/ppermute | solution.py:37
  124.4 2.4 %convolution_convert_fusion.refs_3_ = bf16[256,512]{1,0:T(8,128)(2,1)S(1)} fusion(bf16[256,4096]{1,0:T(8,128)(2,1)S(1)} %collective-permute-done.14, bf16[4096,256]{1,0:T(8,128)(2,1)S(1)} %collective-permute-done.11, bf16[4096,128]{1,0:T(8,128)(2,1)S(1)} %bitcast.15, bf16[4096,128]{1,0:T(8,128)(2,1)S(1)} %bitcast.20), kind=kOutput, calls=%fused_computation.7 | convolution fusion | flops 1086455808 | bytes 6553600 | tf_op jit(solution)/shard_map/dot_general | solution.py:162
  126.7 1.7 %collective-permute-done.13 = bf16[256,4096]{1,0:T(8,128)(2,1)S(1)} collective-permute-done((bf16[256,4096]{1,0:T(8,128)(2,1)}, bf16[256,4096]{1,0:T(8,128)(2,1)S(1)}, u32[]{:S(2)}, u32[]{:S(2)}) %collective-permute-start.13) | collective-permute-done | bytes 2097184 | tf_op jit(solution)/shard_map/ppermute | solution.py:37
  128.5 2.4 %convolution_convert_fusion.1.refs_2_ = bf16[256,512]{1,0:T(8,128)(2,1)S(1)} fusion(bf16[256,4096]{1,0:T(8,128)(2,1)S(1)} %collective-permute-done.13, bf16[4096,256]{1,0:T(8,128)(2,1)S(1)} %collective-permute-done.11, bf16[4096,128]{1,0:T(8,128)(2,1)S(1)} %bitcast.16, bf16[4096,128]{1,0:T(8,128)(2,1)S(1)} %bitcast.21), kind=kOutput, calls=%fused_computation.8 | convolution fusion | flops 1086455808 | bytes 6553600 | tf_op jit(solution)/shard_map/dot_general | solution.py:162
  130.9 0.0 collective-permute-done
  130.9 0.0 all-gather.2.cloned.1.call-done
  130.9 4.2 %fusion.4.query_ref = bf16[512,256]{1,0:T(8,128)(2,1)S(1)} fusion(bf16[512,4096]{1,0:T(8,128)(2,1)} %all-gather.2.cloned.1.call-done, bf16[4096,128]{1,0:T(8,128)(2,1)} %collective-permute-done, bf16[4096,128]{1,0:T(8,128)(2,1)} %bitcast.27), kind=kOutput, calls=%fused_computation.6 | convolution fusion | flops 1078067200 | bytes 6553600 | tf_op jit(solution)/shard_map/dot_general | solution.py:161
  135.1 0.0 collective-permute-done.12
  135.1 2.9 %convolution_convert_fusion.2.refs_1_ = bf16[256,512]{1,0:T(8,128)(2,1)S(1)} fusion(bf16[256,4096]{1,0:T(8,128)(2,1)} %collective-permute-done.12, bf16[4096,256]{1,0:T(8,128)(2,1)S(1)} %copy-done.5, bf16[4096,128]{1,0:T(8,128)(2,1)S(1)} %bitcast.17, bf16[4096,128]{1,0:T(8,128)(2,1)S(1)} %bitcast.22), kind=kOutput, calls=%fused_computation.9 | convolution fusion | flops 1086455808 | bytes 6553600 | tf_op jit(solution)/shard_map/dot_general | solution.py:162
  138.0 2.8 %shard_map.65 = (f32[512,256]{1,0:T(8,128)S(1)}, f32[512,256]{1,0:T(8,128)S(1)}) custom-call(bf16[512,256]{1,0:T(8,128)(2,1)S(1)} %fusion.4.query_ref, bf16[256,512]{1,0:T(8,128)(2,1)S(1)} %convolution_convert_fusion.3.refs_0_, bf16[256,512]{1,0:T(8,128)(2,1)S(1)} %convolution_convert_fusion.2.refs_1_, ...), custom_call_target="tpu_custom_call" | custom-call | flops 536870912 | bytes 2359296 | tf_op jit(solution)/shard_map/pallas_call | solution.py:117
  140.8 1.9 %collective-permute-start.15 = (f32[512,256]{1,0:T(8,128)S(1)}, f32[512,256]{1,0:T(8,128)S(1)}, u32[]{:S(2)}, u32[]{:S(2)}) collective-permute-start(f32[512,256]{1,0:T(8,128)S(1)} %get-tuple-element.18), channel_id=1, source_target_pairs={{0,1},{1,0},{2,3},{3,2},{4,5},{5,4},{6,7},{7,6},{8,9},{9,8},{10,11... | collective-permute-start | bytes 1572872 | tf_op jit(solution)/shard_map/ppermute | solution.py:37
  142.8 1.9 %collective-permute-done.15 = f32[512,256]{1,0:T(8,128)S(1)} collective-permute-done((f32[512,256]{1,0:T(8,128)S(1)}, f32[512,256]{1,0:T(8,128)S(1)}, u32[]{:S(2)}, u32[]{:S(2)}) %collective-permute-start.15) | collective-permute-done | bytes 524320 | tf_op jit(solution)/shard_map/ppermute | solution.py:37
  144.6 0.5 fusion.15
  145.1 0.3 fusion.13
  145.4 11.8 %all_to_all.5 = bf16[32,16,128]{2,1,0:T(8,128)(2,1)S(1)} all-to-all(bf16[32,16,128]{2,1,0:T(8,128)(2,1)S(1)} %bitcast.23), channel_id=1, replica_groups=mesh['x'=4,'zh'=4,'zl'=4,'y'=4,'core'=2] {'zl','y','core'}, dimensions={0} | all-to-all | bytes 262144 | tf_op jit(solution)/shard_map/all_to_all | solution.py:177
  157.2 0.7 reshape.7
  (9 shorter events, 0.1 us)
Async XLA Ops:
  6.5 124.4 %all-gather.2.cloned.1.call-start = ((), (), s32[]{:S(2)}) async-start(), calls=%async_computation.1 | async-start | bytes 4325376 | tf_op jit(solution)/shard_map/all_gather | solution.py:144
  6.5 0.9 copy-start
  7.4 0.7 copy-start.1
  10.0 8.1 %collective-permute-start.3 = (bf16[16,4096]{1,0:T(8,128)(2,1)S(1)}, bf16[16,4096]{1,0:T(8,128)(2,1)S(1)}, u32[]{:S(2)}, u32[]{:S(2)}) collective-permute-start(bf16[16,4096]{1,0:T(8,128)(2,1)S(1)} %get-tuple-element.24), channel_id=1, source_target_pairs={{0,256},{1,257},{2,258},{3,259},{4,260},{5,261},{6,262},{7,263},{8... | collective-permute-start | bytes 393224 | tf_op jit(solution)/shard_map/ppermute | solution.py:37
  15.5 3.3 %collective-permute-start.2 = (bf16[16,4096]{1,0:T(8,128)(2,1)S(1)}, bf16[16,4096]{1,0:T(8,128)(2,1)S(1)}, u32[]{:S(2)}, u32[]{:S(2)}) collective-permute-start(bf16[16,4096]{1,0:T(8,128)(2,1)S(1)} %get-tuple-element.25), channel_id=1, source_target_pairs={{0,128},{1,129},{2,130},{3,131},{4,132},{5,133},{6,134},{7,135},{8... | collective-permute-start | bytes 393224 | tf_op jit(solution)/shard_map/ppermute | solution.py:37
  16.8 3.2 %collective-permute-start.1 = (bf16[16,4096]{1,0:T(8,128)(2,1)S(1)}, bf16[16,4096]{1,0:T(8,128)(2,1)S(1)}, u32[]{:S(2)}, u32[]{:S(2)}) collective-permute-start(bf16[16,4096]{1,0:T(8,128)(2,1)S(1)} %get-tuple-element.26), channel_id=1, source_target_pairs={{0,384},{1,385},{2,386},{3,387},{4,388},{5,389},{6,390},{7,391},{8... | collective-permute-start | bytes 393224 | tf_op jit(solution)/shard_map/ppermute | solution.py:37
  21.0 14.9 %collective-permute-start.4 = (bf16[16,4096]{1,0:T(8,128)(2,1)S(1)}, bf16[16,4096]{1,0:T(8,128)(2,1)S(1)}, u32[]{:S(2)}, u32[]{:S(2)}) collective-permute-start(bf16[16,4096]{1,0:T(8,128)(2,1)S(1)} %select_select_fusion), channel_id=1, source_target_pairs={{0,32},{1,97},{2,34},{3,99},{4,36},{5,101},{6,38},{7,103},{8,40},{... | collective-permute-start | bytes 393224 | tf_op jit(solution)/shard_map/ppermute | solution.py:37
  35.9 4.3 %collective-permute-start.5 = (bf16[16,4096]{1,0:T(8,128)(2,1)S(1)}, bf16[16,4096]{1,0:T(8,128)(2,1)S(1)}, u32[]{:S(2)}, u32[]{:S(2)}) collective-permute-start(bf16[16,4096]{1,0:T(8,128)(2,1)S(1)} %broadcast_select_fusion), channel_id=1, source_target_pairs={{0,96},{1,33},{2,98},{3,35},{4,100},{5,37},{6,102},{7,39},{8,104},... | collective-permute-start | bytes 393224 | tf_op jit(solution)/shard_map/ppermute | solution.py:37
  40.9 11.6 %collective-permute-start.6 = (bf16[16,4096]{1,0:T(8,128)(2,1)S(1)}, bf16[16,4096]{1,0:T(8,128)(2,1)S(1)}, u32[]{:S(2)}, u32[]{:S(2)}) collective-permute-start(bf16[16,4096]{1,0:T(8,128)(2,1)S(1)} %get-tuple-element.23), channel_id=1, source_target_pairs={{0,276},{1,373},{2,278},{3,375},{4,272},{5,369},{6,274},{7,371},{8... | collective-permute-start | bytes 393224 | tf_op jit(solution)/shard_map/ppermute | solution.py:37
  52.5 15.1 %collective-permute-start.7 = (bf16[32,4096]{1,0:T(8,128)(2,1)S(1)}, bf16[32,4096]{1,0:T(8,128)(2,1)S(1)}, u32[]{:S(2)}, u32[]{:S(2)}) collective-permute-start(bf16[32,4096]{1,0:T(8,128)(2,1)S(1)} %pad_maximum_fusion.3), channel_id=1, source_target_pairs={{0,250},{1,399},{2,252},{3,393},{4,254},{5,395},{6,248},{7,397},{8... | collective-permute-start | bytes 786440 | tf_op jit(solution)/shard_map/ppermute | solution.py:37
  55.8 47.3 %copy-start.6 = (bf16[1,4096,128]{2,1,0:T(8,128)(2,1)S(1)}, bf16[1,4096,128]{2,1,0:T(8,128)(2,1)}, u32[]{:S(2)}) copy-start(bf16[1,4096,128]{2,1,0:T(8,128)(2,1)} %param.9) | copy-start | bytes 3145732
  55.8 51.1 %copy-start.2 = (bf16[1,4096,128]{2,1,0:T(8,128)(2,1)S(1)}, bf16[1,4096,128]{2,1,0:T(8,128)(2,1)}, u32[]{:S(2)}) copy-start(bf16[1,4096,128]{2,1,0:T(8,128)(2,1)} %param.11) | copy-start | bytes 3145732
  55.8 51.1 %copy-start.3 = (bf16[1,4096,128]{2,1,0:T(8,128)(2,1)S(1)}, bf16[1,4096,128]{2,1,0:T(8,128)(2,1)}, u32[]{:S(2)}) copy-start(bf16[1,4096,128]{2,1,0:T(8,128)(2,1)} %param.10) | copy-start | bytes 3145732
  57.7 49.1 %collective-permute-start.11 = (bf16[4096,256]{1,0:T(8,128)(2,1)S(1)}, bf16[4096,256]{1,0:T(8,128)(2,1)S(1)}, u32[]{:S(2)}, u32[]{:S(2)}) collective-permute-start(bf16[4096,256]{1,0:T(8,128)(2,1)S(1)} %pad_maximum_fusion.1), channel_id=1, source_target_pairs={{0,1},{1,0},{2,3},{3,2},{4,5},{5,4},{6,7},{7,6},{8,9},{9,8},{10,11... | collective-permute-start | bytes 6291464 | tf_op jit(solution)/shard_map/ppermute | solution.py:37
  67.6 16.3 %collective-permute-start.8 = (bf16[64,4096]{1,0:T(8,128)(2,1)S(1)}, bf16[64,4096]{1,0:T(8,128)(2,1)S(1)}, u32[]{:S(2)}, u32[]{:S(2)}) collective-permute-start(bf16[64,4096]{1,0:T(8,128)(2,1)S(1)} %pad_maximum_fusion.2), channel_id=1, source_target_pairs={{0,136},{1,505},{2,138},{3,507},{4,140},{5,509},{6,142},{7,511},{8... | collective-permute-start | bytes 1572872 | tf_op jit(solution)/shard_map/ppermute | solution.py:37
  70.3 23.5 %collective-permute-start.10 = (bf16[64,4096]{1,0:T(8,128)(2,1)S(1)}, bf16[64,4096]{1,0:T(8,128)(2,1)S(1)}, u32[]{:S(2)}, u32[]{:S(2)}) collective-permute-start(bf16[64,4096]{1,0:T(8,128)(2,1)S(1)} %pad_maximum_fusion.2), channel_id=1, source_target_pairs={{0,4},{1,5},{2,6},{3,7},{4,0},{5,1},{6,2},{7,3},{8,12},{9,13},{10,... | collective-permute-start | bytes 1572872 | tf_op jit(solution)/shard_map/ppermute | solution.py:37
  79.4 13.2 %collective-permute-start.9 = (bf16[64,4096]{1,0:T(8,128)(2,1)S(1)}, bf16[64,4096]{1,0:T(8,128)(2,1)S(1)}, u32[]{:S(2)}, u32[]{:S(2)}) collective-permute-start(bf16[64,4096]{1,0:T(8,128)(2,1)S(1)} %pad_maximum_fusion.2), channel_id=1, source_target_pairs={{0,504},{1,137},{2,506},{3,139},{4,508},{5,141},{6,510},{7,143},{8... | collective-permute-start | bytes 1572872 | tf_op jit(solution)/shard_map/ppermute | solution.py:37
  94.7 29.7 %collective-permute-start.14 = (bf16[256,4096]{1,0:T(8,128)(2,1)}, bf16[256,4096]{1,0:T(8,128)(2,1)S(1)}, u32[]{:S(2)}, u32[]{:S(2)}) collective-permute-start(bf16[256,4096]{1,0:T(8,128)(2,1)} %constant_dynamic-update-slice_fusion), channel_id=1, source_target_pairs={{0,8},{1,121},{2,10},{3,123},{4,12},{5,125},{6,14},{7,127},{8,16},... | collective-permute-start | bytes 6291464 | tf_op jit(solution)/shard_map/ppermute | solution.py:37
  101.1 27.4 %collective-permute-start.13 = (bf16[256,4096]{1,0:T(8,128)(2,1)}, bf16[256,4096]{1,0:T(8,128)(2,1)S(1)}, u32[]{:S(2)}, u32[]{:S(2)}) collective-permute-start(bf16[256,4096]{1,0:T(8,128)(2,1)} %constant_dynamic-update-slice_fusion), channel_id=1, source_target_pairs={{0,2},{1,7},{2,4},{3,1},{4,6},{5,3},{6,0},{7,5},{8,10},{9,15},{10,... | collective-permute-start | bytes 6291464 | tf_op jit(solution)/shard_map/ppermute | solution.py:37
  103.0 27.8 %collective-permute-start = (bf16[4096,128]{1,0:T(8,128)(2,1)S(1)}, bf16[4096,128]{1,0:T(8,128)(2,1)}, u32[]{:S(2)}, u32[]{:S(2)}) collective-permute-start(bf16[4096,128]{1,0:T(8,128)(2,1)S(1)} %bitcast.28), channel_id=1, source_target_pairs={{0,1},{1,0},{2,3},{3,2},{4,5},{5,4},{6,7},{7,6},{8,9},{9,8},{10,11... | collective-permute-start | bytes 3145736 | tf_op jit(solution)/shard_map/ppermute | solution.py:37
  105.0 30.1 %collective-permute-start.12 = (bf16[256,4096]{1,0:T(8,128)(2,1)}, bf16[256,4096]{1,0:T(8,128)(2,1)}, u32[]{:S(2)}, u32[]{:S(2)}) collective-permute-start(bf16[256,4096]{1,0:T(8,128)(2,1)} %constant_dynamic-update-slice_fusion), channel_id=1, source_target_pairs={{0,128},{1,385},{2,130},{3,387},{4,132},{5,389},{6,134},{7,391},{8... | collective-permute-start | bytes 6291464 | tf_op jit(solution)/shard_map/ppermute | solution.py:37
  106.9 21.6 %copy-start.4 = (bf16[4096,256]{1,0:T(8,128)(2,1)}, bf16[4096,256]{1,0:T(8,128)(2,1)S(1)}, u32[]{:S(2)}) copy-start(bf16[4096,256]{1,0:T(8,128)(2,1)S(1)} %collective-permute-done.11) | copy-start | bytes 6291460
  130.9 4.2 %copy-start.5 = (bf16[4096,256]{1,0:T(8,128)(2,1)S(1)}, bf16[4096,256]{1,0:T(8,128)(2,1)}, u32[]{:S(2)}) copy-start(bf16[4096,256]{1,0:T(8,128)(2,1)} %copy-done.4) | copy-start | bytes 6291460
  140.8 3.8 %collective-permute-start.15 = (f32[512,256]{1,0:T(8,128)S(1)}, f32[512,256]{1,0:T(8,128)S(1)}, u32[]{:S(2)}, u32[]{:S(2)}) collective-permute-start(f32[512,256]{1,0:T(8,128)S(1)} %get-tuple-element.18), channel_id=1, source_target_pairs={{0,1},{1,0},{2,3},{3,2},{4,5},{5,4},{6,7},{7,6},{8,9},{9,8},{10,11... | collective-permute-start | bytes 1572872 | tf_op jit(solution)/shard_map/ppermute | solution.py:37
Sparse Core Ops, SparseCore 0:
  26.5 71.7 all-gather.1
